TPU v7x, 32 devices: a whole 2x2x4 slice. The times are simulated.
32 devices in a mesh: section: 8 (over y, x, core), expert: 4 (over z).
Axes of the slice: x: 2, y: 2, z: 4, core: 2. Of those that a mesh axis runs over, the one named last changes fastest.
Arguments:
- resid: bfloat16 [384, 6144], P('expert', 'section'), may hold values from -6 to 6
- query: bfloat16 [384, 6144], P('section', 'expert'), may hold values from -300 to 300, as said below
- new_keys: bfloat16 [384, 1024], P('section', 'expert'), may hold values from -6 to 6
- new_values: bfloat16 [384, 1024], P('section', 'expert'), may hold values from -6 to 6
- cache_keys: bfloat16 [64, 1024, 1024], P('section', None, 'expert'), may hold values from -6 to 6
- cache_values: bfloat16 [64, 1024, 1024], P('section', None, 'expert'), may hold values from -6 to 6
- cache_len: int32 [64], P('section'), may hold values from 1 to 1024, as said below
- out_weight: bfloat16 [6144, 6144], P('expert', 'section'), may hold values from -0.078125 to 0.078125
- expert_ids: int32 [384, 2], replicated, may hold values from 0 to 3, all different within a row; in each aligned block of 96 rows (0 to 95, 96 to 191, ...) at most 60 rows name the same one
- gates: float32 [384, 2], P('expert'), may hold values from 0.05 to 0.95, as said below
- w_gate: bfloat16 [4, 6144, 8192], P('expert', None, 'section'), may hold values from -0.078125 to 0.078125
- w_up: bfloat16 [4, 6144, 8192], P('expert', None, 'section'), may hold values from -0.078125 to 0.078125
- w_down: bfloat16 [4, 8192, 6144], P('expert', 'section'), may hold values from -0.0625 to 0.0625
Outputs:
- layer_out: bfloat16 [384, 6144], P('expert', 'section')
Inputs may be any that keep to these rules, and one draw needn't show every extreme that they name: `query`: some queries may be far larger than typical. `cache_len`: at least one request's cache holds all 1024 positions. `expert_ids`: each row names two different experts; in each aligned block of 96 rows no expert is named by more than 60 rows. `gates`: the two gate weights of a row are positive and sum to one.
All inputs are finite; a program needn't handle non-finite values.
Results may differ from a plain program's by a relative error of at most 0.0055.
Values may be sent and summed in bfloat16 or wider, within the bound.
No kernel may reach another device: no remote copies, remote signals or barrier semaphores. Data moves between devices by JAX's collectives and lax.ppermute only.
A program may use at most 128 MiB of HBM per device.

v0:
```python
import math

import jax
import jax.numpy as jnp
from jax import lax
from jax.sharding import PartitionSpec as P

HQ = 48
KV = 8
HD = 128
TOP = 2


def attend(query, new_keys, new_values, cache_keys, cache_values, cache_len):
    requests = cache_keys.shape[0]
    cache_size = cache_keys.shape[1]
    kv_heads = cache_keys.shape[2] // HD
    groups = HQ // KV
    drafts = query.shape[0] // requests
    scale = 1.0 / math.sqrt(HD)
    queries = query.reshape(requests, drafts, kv_heads, groups, HD)
    past_k = cache_keys.reshape(requests, cache_size, kv_heads, HD)
    past_v = cache_values.reshape(requests, cache_size, kv_heads, HD)
    new_k = new_keys.reshape(requests, drafts, kv_heads, HD)
    new_v = new_values.reshape(requests, drafts, kv_heads, HD)
    past_scores = (
        jnp.einsum("rdkgh,rckh->rkgdc", queries, past_k, preferred_element_type=jnp.float32) * scale
    )
    valid = jnp.arange(cache_size, dtype=jnp.int32)[None, :] < cache_len[:, None]
    past_scores = jnp.where(valid[:, None, None, None, :], past_scores, -1e30)
    new_scores = (
        jnp.einsum("rdkgh,rekh->rkgde", queries, new_k, preferred_element_type=jnp.float32) * scale
    )
    causal = jnp.arange(drafts)[:, None] >= jnp.arange(drafts)[None, :]
    new_scores = jnp.where(causal[None, None, None], new_scores, -1e30)
    top_score = jnp.maximum(jnp.max(past_scores, axis=-1), jnp.max(new_scores, axis=-1))
    past_exp = jnp.exp(past_scores - top_score[..., None])
    new_exp = jnp.exp(new_scores - top_score[..., None])
    total = jnp.sum(past_exp, axis=-1) + jnp.sum(new_exp, axis=-1)
    past_prob = (past_exp / total[..., None]).astype(jnp.bfloat16)
    new_prob = (new_exp / total[..., None]).astype(jnp.bfloat16)
    mixed = jnp.einsum("rkgdc,rckh->rdkgh", past_prob, past_v, preferred_element_type=jnp.float32)
    mixed = mixed + jnp.einsum(
        "rkgde,rekh->rdkgh", new_prob, new_v, preferred_element_type=jnp.float32
    )
    return mixed.reshape(requests * drafts, kv_heads * groups * HD).astype(jnp.bfloat16)


def slot_ranks(flat, experts):
    onehot = (flat[..., None] == jnp.arange(experts, dtype=jnp.int32)).astype(jnp.int32)
    return jnp.sum((jnp.cumsum(onehot, axis=1) - onehot) * onehot, axis=-1)


def per_device(
    resid,
    query,
    new_keys,
    new_values,
    cache_keys,
    cache_values,
    cache_len,
    out_weight,
    expert_ids,
    gates,
    w_gate,
    w_up,
    w_down,
):
    attended = attend(query, new_keys, new_values, cache_keys, cache_values, cache_len)
    gathered = lax.all_gather(attended, "section", axis=0, tiled=True)
    block_rows = resid.shape[0]
    projected = lax.psum_scatter(
        jnp.dot(gathered, out_weight, preferred_element_type=jnp.float32),
        "expert",
        scatter_dimension=0,
        tiled=True,
    )
    hidden_in = (resid.astype(jnp.float32) + projected).astype(jnp.bfloat16)
    experts = lax.axis_size("expert")
    capacity = (block_rows * TOP * 5 + 4 * experts - 1) // (4 * experts)
    slots_total = experts * capacity
    own_index = lax.axis_index("expert")
    own_ids = lax.dynamic_slice_in_dim(expert_ids, own_index * block_rows, block_rows, 0)
    own_flat = own_ids.reshape(1, block_rows * TOP)
    destination = (own_flat * capacity + slot_ranks(own_flat, experts)).reshape(-1)
    slot_iota = jnp.arange(slots_total, dtype=jnp.int32)[:, None]
    everyone = lax.all_gather(hidden_in, "expert", axis=0, tiled=True)
    flat_all = expert_ids.reshape(experts, block_rows * TOP)
    offsets = jnp.arange(experts, dtype=jnp.int32)[:, None] * capacity
    target = jnp.where(flat_all == own_index, offsets + slot_ranks(flat_all, experts), -1).reshape(
        -1
    )
    picker = (
        (target[None, :] == slot_iota)
        .reshape(slots_total, experts * block_rows, TOP)
        .sum(-1)
        .astype(jnp.bfloat16)
    )
    received = jnp.dot(picker, everyone, preferred_element_type=jnp.float32).astype(jnp.bfloat16)
    gate_local = w_gate[0]
    up_local = w_up[0]
    down_local = w_down[0]
    piece = lax.all_gather(received, "section", axis=1, tiled=True)
    gate_acc = jnp.dot(piece, gate_local, preferred_element_type=jnp.float32)
    up_acc = jnp.dot(piece, up_local, preferred_element_type=jnp.float32)
    activated = (jax.nn.silu(gate_acc) * up_acc).astype(jnp.bfloat16)
    partial_out = jnp.dot(activated, down_local, preferred_element_type=jnp.float32)
    summed = lax.psum_scatter(partial_out, "section", scatter_dimension=1, tiled=True)
    returned = lax.all_to_all(
        summed.reshape(experts, capacity, -1), "expert", split_axis=0, concat_axis=0, tiled=True
    )
    returned = returned.reshape(slots_total, -1)
    picked = returned[destination].reshape(block_rows, TOP, -1)
    mixture = jnp.sum(gates[:, :, None] * picked, axis=1)
    return (hidden_in.astype(jnp.float32) + mixture).astype(jnp.bfloat16)


def solution(mesh):
    in_specs = (
        P("expert", "section"),
        P("section", "expert"),
        P("section", "expert"),
        P("section", "expert"),
        P("section", None, "expert"),
        P("section", None, "expert"),
        P("section"),
        P("expert", "section"),
        P(),
        P("expert", None),
        P("expert", None, "section"),
        P("expert", None, "section"),
        P("expert", "section", None),
    )
    out_specs = P("expert", "section")
    return jax.shard_map(
        per_device, mesh=mesh, in_specs=in_specs, out_specs=out_specs, check_vma=False
    )
```

profile of v0, /device:TPU:0, one launch (start us, length us, event | category | flops | bytes accessed | tf_op | source)
XLA Modules:
  0.0 267.7 jit_solution(9538358447341721424)
XLA Ops:
  6.5 0.9 iota_compare_fusion.1
  7.4 1.1 reshape.256
  8.5 0.0 copy-start.4
  8.5 6.9 %reshape.255 = bf16[8,1024,2,128]{3,2,1,0:T(2,128)(2,1)} reshape(bf16[8,1024,256]{2,1,0:T(8,128)(2,1)} %param.17) | data formatting | bytes 8388608 | tf_op jit(solution)/shard_map/reshape | solution.py:22
  15.5 3.8 %bitcast_reduce_fusion = (f32[8,2,6,6]{2,3,1,0:T(8,128)S(1)}, f32[8,2,1024,6,6]{2,4,3,1,0:T(8,128)S(1)}) fusion(pred[8,1024]{1,0:T(8,128)(4,1)S(1)} %iota_compare_fusion.1, bf16[8,6,2,6,128]{4,3,2,1,0:T(8,128)(2,1)S(1)} %reshape.256, bf16[8,1024,2,128,1]{3,2,1,0,4:T(2,128)(2,1)} %bitcast.61), kind=kOutput, calls=%fused_computation.12 | convolution fusion | flops 152763840 | bytes 6711552 | tf_op jit(solution)/shard_map/rdkgh,rckh->rkgdc/dot_general | solution.py:27
  19.3 1.0 fusion.43
  20.3 0.7 copy-done.2
  21.0 1.0 fusion.11
  22.0 0.2 fusion.27
  22.2 0.0 copy-start.5
  22.2 6.9 %reshape.258 = bf16[8,1024,2,128]{3,2,1,0:T(2,128)(2,1)} reshape(bf16[8,1024,256]{2,1,0:T(8,128)(2,1)} %param.18) | data formatting | bytes 8388608 | tf_op jit(solution)/shard_map/reshape | solution.py:23
  29.2 4.9 %fusion.6 = f32[8,2,6,6,128]{4,2,3,1,0:T(8,128)S(1)} fusion(bf16[8,1024,2,128,1]{3,2,1,0,4:T(2,128)(2,1)} %bitcast.60, f32[8,2,1024,6,6]{2,4,3,1,0:T(8,128)} %copy-done.2, f32[8,2,6,6]{2,3,1,0:T(8,128)S(1)} %add.72, f32[8,2,6,6]{2,3,1,0:T(8,128)S(1)} %max.7, pred[8,1024]{1,0:T(8,128)(4,1)S(1)} %iota_compare_fusion.1), kind=kOutput, calls=%fused_computation.7 | convolution fusion | flops 153944064 | bytes 6861312 | tf_op jit(solution)/shard_map/rkgdc,rckh->rdkgh/dot_general | solution.py:42
  34.1 0.3 fusion.26
  34.4 0.8 convert_element_type.59
  35.3 0.0 all-gather.3.cloned.1.call-update
  35.3 0.0 copy-start.6
  35.3 0.0 copy-start.3
  35.3 0.0 reduce-scatter.3.cloned.1.call-start
  35.4 26.8 %all-gather.3.cloned.1.call-done = bf16[384,1536]{1,0:T(8,128)(2,1)} async-done(((bf16[48,1536]{1,0:T(8,128)(2,1)}), bf16[384,1536]{1,0:T(8,128)(2,1)}) %all-gather.3.cloned.1.call-update) | async-done | bytes 1179664 | tf_op jit(solution)/shard_map/all_gather | solution.py:70
  62.2 3.4 %fusion.44 = f32[384,768]{1,0:T(8,128)} fusion(bf16[384,1536]{1,0:T(8,128)(2,1)} %all-gather.3.cloned.1.call-done, bf16[1536,768]{1,0:T(8,128)(2,1)S(1)} %copy-done), kind=kOutput, calls=%fused_computation.73 | convolution fusion | flops 905969664 | bytes 4718592 | tf_op jit(solution)/shard_map/dot_general | solution.py:73
  65.6 0.0 reduce-scatter.3.cloned.1.call-update
  65.6 0.0 all-gather.5.cloned.1.call-start
  65.6 0.1 copy.77
  65.8 0.2 eq.75
  66.0 4.8 %reduce-window.14 = s32[4,4,2,128]{3,2,1,0:T(2,128)S(1)} reduce-window(s32[4,4,2,128]{3,2,1,0:T(2,128)S(1)} %reshape.270, s32[]{:T(128)} %constant.11.clone.1), window={size=1x1x1x128 pad=0_0x0_0x0_0x127_0}, to_apply=%region_5.6 | reduce-window | flops 520192 | bytes 32772 | tf_op jit(solution)/shard_map/reduce-window
  70.8 0.1 slice.26
  70.9 0.1 copy.78
  71.1 0.1 copy.79
  71.2 0.1 broadcast_add_fusion
  71.3 0.2 reduce_sum.61
  71.5 0.1 copy.80
  71.6 0.1 add.75
  71.7 0.1 add.76
  71.8 0.1 convert_reduce_fusion
  71.9 23.0 %reduce-scatter.3.cloned.1.call-done = f32[96,768]{1,0:T(8,128)} async-done(((f32[384,768]{1,0:T(8,128)}), f32[96,768]{1,0:T(8,128)}) %reduce-scatter.3.cloned.1.call-update) | async-done | bytes 294928 | tf_op jit(solution)/shard_map/reduce_scatter | solution.py:72
  94.9 1.0 add_convert_fusion.1
  95.9 16.4 %all_gather.10 = bf16[384,768]{1,0:T(8,128)(2,1)S(1)} all-gather(bf16[96,768]{1,0:T(8,128)(2,1)S(1)} %add_convert_fusion.1), channel_id=1, replica_groups=mesh['section'=8,'expert'=4] {'expert'}, dimensions={0}, use_global_device_ids=true | all-gather | bytes 737280 | tf_op jit(solution)/shard_map/all_gather | solution.py:87
  112.3 1.1 convolution_convert_fusion
  113.4 0.0 all-gather.5.cloned.1.call-update
  113.4 0.2 reduce-scatter.5.cloned.1.call-start
  113.6 29.8 %all-gather.5.cloned.1.call-done = bf16[240,6144]{1,0:T(8,128)(2,1)} async-done(((bf16[240,768]{1,0:T(8,128)(2,1)}), bf16[240,6144]{1,0:T(8,128)(2,1)}) %all-gather.5.cloned.1.call-update) | async-done | bytes 2949136 | tf_op jit(solution)/shard_map/all_gather | solution.py:103
  143.4 7.2 %fusion.4 = f32[240,1024]{1,0:T(8,128)S(1)} fusion(bf16[240,6144]{1,0:T(8,128)(2,1)} %all-gather.5.cloned.1.call-done, bf16[1,6144,1024]{2,1,0:T(8,128)(2,1)} %param.23), kind=kOutput, calls=%fused_computation.5 | convolution fusion | flops 3019898880 | bytes 16515072 | tf_op jit(solution)/shard_map/dot_general | solution.py:104
  150.6 17.9 %fusion = f32[240,6144]{1,0:T(8,128)} fusion(bf16[1,1024,6144]{2,1,0:T(8,128)(2,1)} %param.25, bf16[240,6144]{1,0:T(8,128)(2,1)} %all-gather.5.cloned.1.call-done, bf16[1,6144,1024]{2,1,0:T(8,128)(2,1)} %param.24, f32[240,1024]{1,0:T(8,128)S(1)} %fusion.4), kind=kOutput, calls=%fused_computation.1 | convolution fusion | flops 6041272320 | bytes 34996224 | tf_op jit(solution)/shard_map/dot_general | solution.py:107
  168.5 0.0 reduce-scatter.5.cloned.1.call-update
  168.5 0.1 broadcast_multiply_fusion
  168.6 0.1 copy.82
  168.7 0.1 eq.85
  168.8 59.5 %reduce-scatter.5.cloned.1.call-done = f32[240,768]{1,0:T(8,128)} async-done(((f32[240,6144]{1,0:T(8,128)}), f32[240,768]{1,0:T(8,128)}) %reduce-scatter.5.cloned.1.call-update) | async-done | bytes 737296 | tf_op jit(solution)/shard_map/reduce_scatter | solution.py:108
  228.3 2.1 reshape.262
  230.4 4.6 %all-to-all-start = ((f32[4,60,768]{2,1,0:T(8,128)}), f32[4,60,768]{2,1,0:T(8,128)}, u32[]{:S(2)}, u32[]{:S(2)}) async-start(f32[4,60,768]{2,1,0:T(8,128)} %reshape.262), calls=%async_computation.2 | async-start | bytes 1572864 | tf_op jit(solution)/shard_map/all_to_all | solution.py:109
  235.0 1.2 reduce-window.16
  236.2 0.1 slice.29
  236.3 0.1 copy.83
  236.4 0.1 copy.84
  236.5 0.1 broadcast.131
  236.6 0.1 copy.81
  236.7 0.1 mul.80
  236.9 0.1 copy.76
  237.0 18.1 %all-to-all-done = f32[4,60,768]{2,1,0:T(8,128)} async-done(((f32[4,60,768]{2,1,0:T(8,128)}), f32[4,60,768]{2,1,0:T(8,128)}, u32[]{:S(2)}, u32[]{:S(2)}) %all-to-all-start) | async-done | bytes 737312 | tf_op jit(solution)/shard_map/all_to_all | solution.py:109
  255.2 1.4 reshape.263
  256.5 1.8 gather_fusion
  258.3 1.4 reshape.269
  259.7 0.8 multiply_reduce_fusion
  260.5 0.7 add_convert_fusion
  (38 shorter events, 0.4 us)
Async XLA Ops:
  6.5 55.7 %copy-start = (bf16[1536,768]{1,0:T(8,128)(2,1)S(1)}, bf16[1536,768]{1,0:T(8,128)(2,1)}, u32[]{:S(2)}) copy-start(bf16[1536,768]{1,0:T(8,128)(2,1)} %param.20) | copy-start | bytes 7077892
  6.5 55.7 %all-gather.3.cloned.1.call-start = ((), (), s32[]{:S(2)}) async-start(), calls=%async_computation.3 | async-start | bytes 1327104 | tf_op jit(solution)/shard_map/all_gather | solution.py:70
  8.5 6.9 %copy-start.4 = (bf16[48,256]{1,0:T(8,128)(2,1)S(1)}, bf16[48,256]{1,0:T(8,128)(2,1)}, u32[]{:S(2)}) copy-start(bf16[48,256]{1,0:T(8,128)(2,1)} %param.15) | copy-start | bytes 73732
  19.3 1.7 copy-start.2
  22.2 6.9 %copy-start.5 = (bf16[48,256]{1,0:T(8,128)(2,1)S(1)}, bf16[48,256]{1,0:T(8,128)(2,1)}, u32[]{:S(2)}) copy-start(bf16[48,256]{1,0:T(8,128)(2,1)} %param.16) | copy-start | bytes 73732
  35.3 30.4 %copy-start.6 = (s32[384,2]{0,1:T(2,128)S(1)}, s32[384,2]{0,1:T(2,128)}, u32[]{:S(2)}) copy-start(s32[384,2]{0,1:T(2,128)} %param.21) | copy-start | bytes 9220
  35.3 59.6 %copy-start.3 = (bf16[96,768]{1,0:T(8,128)(2,1)S(1)}, bf16[96,768]{1,0:T(8,128)(2,1)}, u32[]{:S(2)}) copy-start(bf16[96,768]{1,0:T(8,128)(2,1)} %param.13) | copy-start | bytes 442372
  35.3 59.6 %reduce-scatter.3.cloned.1.call-start = ((), (), s32[]{:S(2)}) async-start(), calls=%async_computation.4 | async-start | bytes 1474560 | tf_op jit(solution)/shard_map/reduce_scatter | solution.py:72
  65.6 77.8 %all-gather.5.cloned.1.call-start = ((), (), s32[]{:S(2)}) async-start(), calls=%async_computation.5 | async-start | bytes 3317760 | tf_op jit(solution)/shard_map/all_gather | solution.py:103
  113.4 114.9 %reduce-scatter.5.cloned.1.call-start = ((), (), s32[]{:S(2)}) async-start(), calls=%async_computation.6 | async-start | bytes 6635520 | tf_op jit(solution)/shard_map/reduce_scatter | solution.py:108
  168.5 68.4 %copy-start.7 = (f32[96,2]{0,1:T(2,128)S(1)}, f32[96,2]{0,1:T(2,128)}, u32[]{:S(2)}) copy-start(f32[96,2]{0,1:T(2,128)} %param.22) | copy-start | bytes 2308
  230.4 24.8 %all-to-all-start = ((f32[4,60,768]{2,1,0:T(8,128)}), f32[4,60,768]{2,1,0:T(8,128)}, u32[]{:S(2)}, u32[]{:S(2)}) async-start(f32[4,60,768]{2,1,0:T(8,128)} %reshape.262), calls=%async_computation.2 | async-start | bytes 1572864 | tf_op jit(solution)/shard_map/all_to_all | solution.py:109
  255.2 6.0 %copy-start.1 = (bf16[1536,768]{1,0:T(8,128)(2,1)S(1)}, bf16[1536,768]{1,0:T(8,128)(2,1)}, u32[]{:S(2)}) copy-start(bf16[1536,768]{1,0:T(8,128)(2,1)} %param.20) | copy-start | bytes 7077892
Sparse Core Ops, SparseCore 0:
  35.4 26.7 all-gather.2
  65.7 29.1 reduce-scatter.2
  113.5 29.8 all-gather.4
  168.6 59.6 reduce-scatter.4
where the time goes:
time: 268 us
  waiting for transfers between devices  157 us (59%)
  matrix products  39.5 us (15%)
  local copies, waits for them, and re-layouts  25.2 us (9%)
  blocking collectives  16.4 us (6%)
  between operations  13.4 us (5%)
  other arithmetic  11 us (4%)
  starting transfers between devices  4.91 us (2%)
    reduce_scatter x1, waiting for transfers between devices, per_device(): lax.psum_scatter(partial_out, 'section', scatter_dimension=1, tiled=True)  59.5 us
    all_gather x1, waiting for transfers between devices, per_device(): piece = lax.all_gather(received, 'section', axis=1, tiled=True)  29.8 us
    all_gather x1, waiting for transfers between devices, per_device(): gathered = lax.all_gather(attended, 'section', axis=0, tiled=True)  26.8 us
    reduce_scatter x1, waiting for transfers between devices, per_device(): lax.psum_scatter(jnp.dot(gathered, out_weight, preferred_element_type=jnp...  23 us
    all_to_all x1, waiting for transfers between devices, per_device(): lax.all_to_all(summed.reshape(experts, capacity, -1), 'expert', split_axi...  18.1 us
    dot_general x1, matrix products, per_device(): jnp.dot(activated, down_local, preferred_element_type=jnp.float32)  17.9 us
    all_gather x1, blocking collectives, per_device(): everyone = lax.all_gather(hidden_in, 'expert', axis=0, tiled=True)  16.4 us
    dot_general x1, matrix products, per_device(): gate_acc = jnp.dot(piece, gate_local, preferred_element_type=jnp.float32)  7.16 us
  transfers between devices with their start and end apart: 5, of which 5 were waited for; matrix products, arithmetic and copies ran while one was open for 3% of the time, Pallas kernels for 0%

commit v1 on v0

v1 whole, which is shorter than its diff:
```python
import functools
import math

import jax
import jax.numpy as jnp
from jax import lax
from jax.experimental import pallas as pl
from jax.experimental.pallas import tpu as pltpu
from jax.sharding import PartitionSpec as P

HQ = 48
KV = 8
HD = 128
TOP = 2
GROUPS = HQ // KV
SCALE = 1.0 / math.sqrt(HD)
MASKED = -1e30
NT = (((1,), (1,)), ((), ()))


def spread(rows, drafts, transposed):
    shape = (rows, rows // drafts * 8) if transposed else (rows // drafts * 8, rows)
    at = lax.broadcasted_iota(jnp.int32, shape, 1 if transposed else 0)
    row = lax.broadcasted_iota(jnp.int32, shape, 0 if transposed else 1)
    inside = at & 7
    return ((inside < drafts) & ((at >> 3) * drafts + inside == row)).astype(jnp.bfloat16)


def attend_kernel(
    drafts, len_hbm, q_hbm, nk_hbm, nv_hbm, ck_hbm, cv_hbm, w_hbm, o_ref, w_ref, *scratch
):
    len_ref, q_ref, nk_ref, nv_ref, ck_ref, cv_ref, qs, scores, acc, sem, k_sem, v_sem, w_sem = scratch
    requests, size, width = ck_ref.shape
    rows = q_ref.shape[0]
    heads = width // HD
    group = GROUPS * 8
    wide = heads * group

    small = [
        pltpu.make_async_copy(src, dst, sem.at[i])
        for i, (src, dst) in enumerate(
            ((q_hbm, q_ref), (len_hbm, len_ref), (nk_hbm, nk_ref), (nv_hbm, nv_ref))
        )
    ]
    keys = [pltpu.make_async_copy(ck_hbm.at[r], ck_ref.at[r], k_sem.at[r]) for r in range(requests)]
    values = [
        pltpu.make_async_copy(cv_hbm.at[r], cv_ref.at[r], v_sem.at[r]) for r in range(requests)
    ]
    part = w_ref.shape[0] // 4
    weights = [
        pltpu.make_async_copy(
            w_hbm.at[i * part : (i + 1) * part], w_ref.at[i * part : (i + 1) * part], w_sem.at[i]
        )
        for i in range(4)
    ]
    for copy in small:
        copy.start()
    for pair in zip(keys, values):
        for copy in pair:
            copy.start()
    for copy in weights:
        copy.start()
    for copy in small:
        copy.wait()
    qs[...] = dot(spread(rows, drafts, False), q_ref[...])

    at = lax.broadcasted_iota(jnp.int32, (wide, rows), 1)
    draft_at = lax.broadcasted_iota(jnp.int32, (wide, rows), 0) & 7
    past_at = lax.broadcasted_iota(jnp.int32, (wide, size), 1)

    def queries(r):
        q_all = qs[r * 8 : (r + 1) * 8, :]
        zero = jnp.zeros((group, HD), jnp.float32)
        parts = []
        for h in range(heads):
            q = jnp.concatenate(
                [
                    q_all[:, (h * GROUPS + g) * HD : (h * GROUPS + g + 1) * HD]
                    for g in range(GROUPS)
                ],
                axis=0,
            )
            parts.append(jnp.concatenate([q if j == h else zero for j in range(heads)], axis=1))
        return jnp.concatenate(parts, axis=0).astype(jnp.bfloat16)

    def score(r):
        past = lax.dot_general(queries(r), ck_ref[r], NT, preferred_element_type=jnp.float32)
        scores[r % 4] = jnp.where(past_at < len_ref[r], past * SCALE, MASKED)

    def mix(r):
        past = scores[r % 4]
        new = lax.dot_general(queries(r), nk_ref[...], NT, preferred_element_type=jnp.float32)
        key_at = at - r * drafts
        new_ok = (key_at >= 0) & (key_at <= draft_at) & (key_at < drafts)
        new = jnp.where(new_ok, new * SCALE, MASKED)
        top = jnp.maximum(
            jnp.max(past, axis=1, keepdims=True), jnp.max(new, axis=1, keepdims=True)
        )
        past = jnp.exp(past - top)
        new = jnp.exp(new - top)
        total = jnp.sum(past, axis=1, keepdims=True) + jnp.sum(new, axis=1, keepdims=True)
        inverse = 1.0 / total
        mixed = dot((past * inverse).astype(jnp.bfloat16), cv_ref[r])
        mixed = mixed + dot((new * inverse).astype(jnp.bfloat16), nv_ref[...])
        for h in range(heads):
            for g in range(GROUPS):
                col = (h * GROUPS + g) * HD
                row = h * group + g * 8
                acc[r * 8 : (r + 1) * 8, col : col + HD] = mixed[
                    row : row + 8, h * HD : (h + 1) * HD
                ]

    pairs = [range(i, min(i + 2, requests)) for i in range(0, requests, 2)]
    for r in pairs[0]:
        keys[r].wait()
    for r in pairs[0]:
        score(r)
    for i, pair in enumerate(pairs):
        following = pairs[i + 1] if i + 1 < len(pairs) else ()
        for r in following:
            keys[r].wait()
        for r in pair:
            values[r].wait()
        for r in following:
            score(r)
        for r in pair:
            mix(r)
    kept = spread(rows, drafts, True)
    o_ref[...] = dot(kept, acc[...].astype(jnp.bfloat16)).astype(jnp.bfloat16)
    for copy in weights:
        copy.wait()


def attend(query, new_keys, new_values, cache_keys, cache_values, cache_len, weight):
    requests, size, width = cache_keys.shape
    rows, q_width = query.shape
    wide = width // HD * GROUPS * 8
    f32, bf16 = jnp.float32, jnp.bfloat16
    operands = [
        pltpu.with_memory_space_constraint(v, pltpu.HBM)
        for v in (cache_len, query, new_keys, new_values, cache_keys, cache_values, weight)
    ]
    return pl.pallas_call(
        functools.partial(attend_kernel, rows // requests),
        in_specs=[pl.BlockSpec(memory_space=pl.ANY)] * len(operands),
        out_specs=[pl.BlockSpec(memory_space=pltpu.VMEM)] * 2,
        out_shape=[
            jax.ShapeDtypeStruct(query.shape, bf16),
            pltpu.VMEM(weight.shape, weight.dtype),
        ],
        scratch_shapes=[
            pltpu.SMEM(cache_len.shape, jnp.int32),
            pltpu.VMEM(query.shape, bf16),
            pltpu.VMEM(new_keys.shape, bf16),
            pltpu.VMEM(new_values.shape, bf16),
            pltpu.VMEM(cache_keys.shape, bf16),
            pltpu.VMEM(cache_values.shape, bf16),
            pltpu.VMEM((requests * 8, q_width), f32),
            pltpu.VMEM((4, wide, size), f32),
            pltpu.VMEM((requests * 8, q_width), f32),
            pltpu.SemaphoreType.DMA((4,)),
            pltpu.SemaphoreType.DMA((requests,)),
            pltpu.SemaphoreType.DMA((requests,)),
            pltpu.SemaphoreType.DMA((4,)),
        ],
        compiler_params=pltpu.CompilerParams(vmem_limit_bytes=20 * 1024 * 1024),
        cost_estimate=pl.CostEstimate(
            flops=4 * rows * size * q_width,
            bytes_accessed=4 * requests * size * width,
            transcendentals=rows * size * q_width // HD,
        ),
        name="attend",
    )(*operands)


def project_kernel(at_ref, *refs):
    pieces, (w_ref, own_ref, *out_refs, scratch) = refs[: at_ref.shape[0]], refs[at_ref.shape[0] :]
    part = pieces[0].shape[0]
    rows = own_ref.shape[0]
    for i, piece in enumerate(pieces):
        scratch[pl.ds(pl.multiple_of(at_ref[i] * part, 16), part), :] = piece[...]
    product = dot(scratch[...], w_ref[...])
    own_ref[...] = product[:rows, :]
    for i, out in enumerate(out_refs):
        out[...] = product[(i + 1) * rows : (i + 2) * rows, :].astype(out.dtype)


def project(places, pieces, weight, blocks):
    part, depth = pieces[0].shape
    width = weight.shape[1]
    rows = part * len(pieces) // blocks
    vmem = pl.BlockSpec(memory_space=pltpu.VMEM)
    own = jax.ShapeDtypeStruct((rows, width), jnp.float32)
    sent = jax.ShapeDtypeStruct((rows, width), jnp.bfloat16)
    return pl.pallas_call(
        project_kernel,
        in_specs=[pl.BlockSpec(memory_space=pltpu.SMEM)] + [vmem] * (len(pieces) + 1),
        out_specs=[vmem] * blocks,
        out_shape=[own] + [sent] * (blocks - 1),
        scratch_shapes=[pltpu.VMEM((part * len(pieces), depth), jnp.bfloat16)],
        compiler_params=pltpu.CompilerParams(vmem_limit_bytes=8 * 1024 * 1024),
        cost_estimate=pl.CostEstimate(
            flops=2 * part * len(pieces) * depth * width,
            bytes_accessed=2 * depth * width,
            transcendentals=0,
        ),
        name="project",
    )(places, *pieces, weight)


def fetch_kernel(dim, count, at_ref, src, *refs):
    parts, sem = refs[-1 - count : -1], refs[-1]
    width = parts[0].shape[dim] // 2
    copies = []
    for i, part in enumerate(parts):
        for side in range(2):
            n = 2 * i + side
            start = pl.multiple_of(at_ref[n] * width, 128)
            here = slice(side * width, (side + 1) * width)
            if dim == 0:
                pair = src.at[0, pl.ds(start, width), :], part.at[here, :]
            else:
                pair = src.at[0, :, pl.ds(start, width)], part.at[:, here]
            copies.append(pltpu.make_async_copy(*pair, sem.at[n]))
    for copy in copies:
        copy.start()
    for copy in copies:
        copy.wait()


def fetch(weight, dim, at, *after):
    count = at.shape[0] // 2
    shape = list(weight.shape[1:])
    shape[dim] //= count
    weight = pltpu.with_memory_space_constraint(weight, pltpu.HBM)
    return pl.pallas_call(
        functools.partial(fetch_kernel, dim, count),
        in_specs=[pl.BlockSpec(memory_space=pltpu.SMEM)]
        + [pl.BlockSpec(memory_space=pl.ANY)] * (1 + len(after)),
        out_specs=[pl.BlockSpec(memory_space=pltpu.VMEM)] * count,
        out_shape=[pltpu.VMEM(tuple(shape), weight.dtype)] * count,
        scratch_shapes=[pltpu.SemaphoreType.DMA((2 * count,))],
        compiler_params=pltpu.CompilerParams(vmem_limit_bytes=1024 * 1024),
        cost_estimate=pl.CostEstimate(
            flops=0, bytes_accessed=2 * math.prod(weight.shape), transcendentals=0
        ),
        name="fetch",
    )(at, weight, *after)


def swap(value, axis, mask):
    size = lax.axis_size(axis)
    return lax.ppermute(value, axis, [(i, i ^ mask) for i in range(size)])


def dot(a, b):
    return jnp.dot(a, b, preferred_element_type=jnp.float32)


def share(value):
    chips = lax.axis_size("section") // 2
    return [value] + [swap(value, "section", 2 * k) for k in range(1, chips)]


def exchange(parts):
    count = lax.axis_size("expert")
    arrived = {k: swap(parts[k], "expert", k) for k in reversed(range(1, count))}
    return [arrived[k] for k in range(1, count)]


def per_device(
    resid,
    query,
    new_keys,
    new_values,
    cache_keys,
    cache_values,
    cache_len,
    out_weight,
    expert_ids,
    gates,
    w_gate,
    w_up,
    w_down,
):
    f32, bf16 = jnp.float32, jnp.bfloat16
    sections = lax.axis_size("section")
    experts = lax.axis_size("expert")
    chips = sections // 2
    section = lax.axis_index("section")
    own = lax.axis_index("expert")
    chip, core = section // 2, section % 2
    block_rows, width = resid.shape
    capacity = (block_rows * TOP * 5 + 4 * experts - 1) // (4 * experts)
    slots = -(-capacity // 16) * 16

    ids = lax.dynamic_slice_in_dim(expert_ids, own * block_rows, block_rows, 0)
    relative = ids ^ own
    order = jnp.arange(experts, dtype=jnp.int32)
    names = relative[:, :, None] == order
    named = jnp.any(names, axis=1)
    row = jnp.arange(block_rows, dtype=jnp.int32)
    earlier = (row[None, :] < row[:, None]).astype(bf16)
    rank = dot(earlier, named.astype(bf16)).astype(jnp.int32)
    slot = jnp.arange(slots, dtype=jnp.int32)
    hit = rank[:, :, None] == slot
    pick = (hit & named[:, :, None]).astype(bf16).reshape(block_rows, experts * slots)
    place = [
        (hit & names[:, k, :, None]).astype(bf16).reshape(block_rows, experts * slots)
        for k in range(TOP)
    ]

    attended, out_weight = attend(
        query, new_keys, new_values, cache_keys, cache_values, cache_len, out_weight
    )
    same = [attended] + [swap(attended, "section", 2 * k) for k in range(1, chips)]
    step = jnp.arange(2 * chips, dtype=jnp.int32)
    found = section ^ step
    block = (step % chips) ^ chip ^ own
    places = block * 2 + (core ^ (step // chips))
    found, places = lax.optimization_barrier((found, places))
    same, gate_parts = lax.optimization_barrier((same, fetch(w_gate, 0, found, attended)))
    other = [swap(v, "section", 1) for v in same]
    projected = list(project(places, same + other, out_weight, experts))
    arrived = exchange(projected)
    hidden, up_parts = lax.optimization_barrier(
        (resid.astype(f32) + projected[0], fetch(w_up, 0, found, projected[0]))
    )
    for part in arrived:
        hidden = hidden + part.astype(f32)
    hidden_in = hidden.astype(bf16)

    buffers = lax.dot_general(
        pick, hidden_in, (((0,), (0,)), ((), ())), preferred_element_type=f32
    ).astype(bf16)
    buffers = buffers.reshape(experts, slots, width)
    early = [k for k in range(1, chips) if k & 2]
    first = {k: swap(buffers[0], "section", 2 * k) for k in early}
    rest = jnp.concatenate(exchange(buffers), axis=0)
    rest, first = lax.optimization_barrier((rest, first))
    received = jnp.concatenate([buffers[0], rest], axis=0)
    second = {k: swap(rest if k in first else received, "section", 2 * k) for k in range(1, chips)}

    sums = []
    for k in range(chips):
        if not k:
            same = received
        elif k in first:
            first[k], second[k], sums = lax.optimization_barrier((first[k], second[k], sums))
            same = jnp.concatenate([first[k], second[k]], axis=0)
        elif k == 1:
            down_parts = fetch(w_down, 1, found, *sums)
            same, sums, down_parts = lax.optimization_barrier((second[k], sums, down_parts))
        else:
            same, sums = lax.optimization_barrier((second[k], sums))
        for side, piece in enumerate((same, swap(same, "section", 1))):
            here = slice(side * width, (side + 1) * width)
            parts = [dot(piece, w[k][here]) for w in (gate_parts, up_parts)]
            sums = [a + b for a, b in zip(sums, parts)] if sums else parts
    gate_acc, up_acc = sums
    activated = (jax.nn.silu(gate_acc) * up_acc).astype(bf16)

    def down(k, side):
        here = slice(side * width, (side + 1) * width)
        return dot(activated, down_parts[k][:, here])

    order = sorted(range(1, chips), key=lambda k: (-(k & 2), -k))
    ahead = {k: down(k, 1).astype(bf16) for k in early}
    later, rest = {}, {}
    for k in order:
        for_core = ahead[k] if k in ahead else down(k, 1).astype(bf16)
        both = (down(k, 0) + swap(for_core, "section", 1).astype(f32)).astype(bf16)
        later[k], rest[k] = both[:slots], both[slots:]
        if k in ahead:
            later[k], rest[k], activated = lax.optimization_barrier((later[k], rest[k], activated))
    rest = {k: swap(rest[k], "section", 2 * k) for k in order}
    total = down(0, 0) + swap(down(0, 1).astype(bf16), "section", 1).astype(f32)
    mine, total = total[:slots], total[slots:]
    for k in order:
        total = total + rest[k].astype(f32)
    total, later = lax.optimization_barrier((total.astype(bf16), later))

    arrived = exchange([None] + jnp.split(total, experts - 1, axis=0))
    later = [swap(later[k], "section", 2 * k) for k in order]
    mine, arrived = lax.optimization_barrier((mine, arrived))
    for part in later:
        mine = mine + part.astype(f32)
    returned = jnp.concatenate([mine.astype(bf16)] + arrived, axis=0)
    mixture = sum(gates[:, k : k + 1] * dot(place[k], returned) for k in range(TOP))
    return (hidden_in.astype(f32) + mixture).astype(bf16)


def solution(mesh):
    in_specs = (
        P("expert", "section"),
        P("section", "expert"),
        P("section", "expert"),
        P("section", "expert"),
        P("section", None, "expert"),
        P("section", None, "expert"),
        P("section"),
        P("expert", "section"),
        P(),
        P("expert", None),
        P("expert", None, "section"),
        P("expert", None, "section"),
        P("expert", "section", None),
    )
    out_specs = P("expert", "section")
    return jax.shard_map(
        per_device, mesh=mesh, in_specs=in_specs, out_specs=out_specs, check_vma=False
    )
```

time: 268 us -> 110 us (0.41)
  waiting for transfers between devices: 157 us -> 31.7 us
  starting transfers between devices: 4.91 us -> 34.9 us
  Pallas kernels: 0 us -> 25.7 us
  local copies, waits for them, and re-layouts: 25.2 us -> 0.31 us
  matrix products: 39.5 us -> 16 us
  blocking collectives: 16.4 us -> 0 us
  between operations: 13.4 us -> 0.47 us
  other arithmetic: 11 us -> 1.24 us
    reduce_scatter x2 -> x0, waiting for transfers between devices: 82.5 us -> none  [the longest x1 59.5 us: per_device(): lax.psum_scatter(partial_out, 'section', scatter_dimension=1, tiled=True)]
    all_gather x2 -> x0, waiting for transfers between devices: 56.6 us -> none  [the longest x1 29.8 us: per_device(): piece = lax.all_gather(received, 'section', axis=1, tiled=True)]
    ppermute x0 -> x35, starting transfers between devices: none -> 34.9 us  [swap(): return lax.ppermute(value, axis, [(i, i ^ mask) for i in range(size)])]
    ppermute x0 -> x35, waiting for transfers between devices: none -> 31.7 us  [swap(): return lax.ppermute(value, axis, [(i, i ^ mask) for i in range(size)])]
    pallas_call x0 -> x5, Pallas kernels: none -> 25.7 us  [the longest x3 15.8 us: fetch(): pl.pallas_call(functools.partial(fetch_kernel, dim, count), in_specs=[pl....]
    dot_general x8 -> x28, matrix products: 39.5 us -> 16 us  [the longest x27 15.7 us: dot(): return jnp.dot(a, b, preferred_element_type=jnp.float32)]
    reshape x8 -> x0, local copies, waits for them, and re-layouts: 19.8 us -> none  [the longest x1 6.93 us: attend(): past_k = cache_keys.reshape(requests, cache_size, kv_heads, HD)]
    all_to_all x1 -> x0, waiting for transfers between devices: 18.1 us -> none  [per_device(): lax.all_to_all(summed.reshape(experts, capacity, -1), 'expert', split_axi...]
  transfers between devices with their start and end apart: 5 -> 35, of which waited for: 5 -> 18; matrix products, arithmetic and copies ran while one was open for 3% -> 11% of each run, Pallas kernels for 0% -> 14%
where the time goes in v1:
time: 110 us
  starting transfers between devices  34.9 us (32%)
  waiting for transfers between devices  31.7 us (29%)
  Pallas kernels  25.7 us (23%)
  matrix products  16 us (15%)
  other arithmetic  1.24 us (1%)
    ppermute x35, starting transfers between devices, swap(): return lax.ppermute(value, axis, [(i, i ^ mask) for i in range(size)])  34.9 us
    ppermute x35, waiting for transfers between devices, swap(): return lax.ppermute(value, axis, [(i, i ^ mask) for i in range(size)])  31.7 us
    pallas_call x3, Pallas kernels, fetch(): pl.pallas_call(functools.partial(fetch_kernel, dim, count), in_specs=[pl....  15.8 us
    dot_general x27, matrix products, dot(): return jnp.dot(a, b, preferred_element_type=jnp.float32)  15.7 us
    pallas_call x1, Pallas kernels, attend(): pl.pallas_call(functools.partial(attend_kernel, rows // requests), in_spe...  8.22 us
  transfers between devices with their start and end apart: 35, of which 18 were waited for; matrix products, arithmetic and copies ran while one was open for 11% of the time, Pallas kernels for 14%

profile of v1, /device:TPU:0, one launch (start us, length us, event | category | flops | bytes accessed | tf_op | source)
XLA Modules:
  0.0 110.2 jit_solution(15938997751598575270)
XLA Ops:
  0.0 8.2 %attend.1 = (bf16[48,1536]{1,0:T(8,128)(2,1)S(1)}, bf16[1536,768]{1,0:T(8,128)(2,1)S(1)}) custom-call(s32[8]{0:T(128)} %len_hbm.1, bf16[48,1536]{1,0:T(8,128)(2,1)} %q_hbm.1, bf16[48,256]{1,0:T(8,128)(2,1)} %nk_hbm.1, bf16[48,256]{1,0:T(8,128)(2,1)} %nv_hbm.1, bf16[8,1024,256]{2,1,0:T(8,128)(2,1)} %ck_hbm.1, bf16[8,1024,256]{2,1,0:T(8,128)(2,1)} %cv_hbm.1, ...), custom_call_target="tpu_custom_call" | custom-call | flops 301989888 | bytes 8388608 | tf_op jit(solution)/shard_map/attend/pallas_call | solution.py:143
  8.2 3.0 %collective-permute-start = (bf16[48,1536]{1,0:T(8,128)(2,1)S(1)}, bf16[48,1536]{1,0:T(8,128)(2,1)S(1)}, u32[]{:S(2)}, u32[]{:S(2)}) collective-permute-start(bf16[48,1536]{1,0:T(8,128)(2,1)S(1)} %get-tuple-element.77.refs_0_), channel_id=1, source_target_pairs={{0,8},{4,12},{8,0},{12,4},{16,24},{20,28},{24,16},{28,20},{1,9},{5... | collective-permute-start | bytes 442376 | tf_op jit(solution)/shard_map/ppermute | solution.py:253
  11.2 1.5 %collective-permute-start.1 = (bf16[48,1536]{1,0:T(8,128)(2,1)S(1)}, bf16[48,1536]{1,0:T(8,128)(2,1)S(1)}, u32[]{:S(2)}, u32[]{:S(2)}) collective-permute-start(bf16[48,1536]{1,0:T(8,128)(2,1)S(1)} %get-tuple-element.77.refs_0_), channel_id=1, source_target_pairs={{0,16},{4,20},{8,24},{12,28},{16,0},{20,4},{24,8},{28,12},{1,17},{... | collective-permute-start | bytes 442376 | tf_op jit(solution)/shard_map/ppermute | solution.py:253
  12.8 0.8 dynamic-slice_xor_fusion
  13.6 5.2 %fetch.3 = (bf16[1536,1024]{1,0:T(8,128)(2,1)S(1)}, bf16[1536,1024]{1,0:T(8,128)(2,1)S(1)}, bf16[1536,1024]{1,0:T(8,128)(2,1)S(1)}, bf16[1536,1024]{1,0:T(8,128)(2,1)S(1)}) custom-call(s32[8]{0:T(128)S(1)} %get-tuple-element.72.at_ref, bf16[1,6144,1024]{2,1,0:T(8,128)(2,1)} %src.3, bf16[48,1536]{1,0:T(8,128)(2,1)S(1)} %get-tuple-element.77.refs_0_), custom_call_target="tpu_custom_call" | custom-call | bytes 12582912 | tf_op jit(solution)/shard_map/fetch/pallas_call | solution.py:236
  19.0 0.7 collective-permute-done.1.refs_2_
  19.7 0.5 collective-permute-start.4
  21.8 1.7 %project.1 = (f32[96,768]{1,0:T(8,128)S(1)}, bf16[96,768]{1,0:T(8,128)(2,1)S(1)}, bf16[96,768]{1,0:T(8,128)(2,1)S(1)}, bf16[96,768]{1,0:T(8,128)(2,1)S(1)}) custom-call(s32[8]{0:T(128)S(1)} %get-tuple-element.70.at_ref, bf16[48,1536]{1,0:T(8,128)(2,1)S(1)} %get-tuple-element.77.refs_0_, bf16[48,1536]{1,0:T(8,128)(2,1)S(1)} %collective-permute-done.refs_1_, ...), custom_call_target="tpu_custom_call" | custom-call | flops 905969664 | bytes 2359296 | tf_op jit(solution)/shard_map/project/pallas_call | solution.py:195
  23.5 1.6 %collective-permute-start.7 = (bf16[96,768]{1,0:T(8,128)(2,1)S(1)}, bf16[96,768]{1,0:T(8,128)(2,1)S(1)}, u32[]{:S(2)}, u32[]{:S(2)}) collective-permute-start(bf16[96,768]{1,0:T(8,128)(2,1)S(1)} %get-tuple-element.88), channel_id=1, source_target_pairs={{0,1},{1,0},{2,3},{3,2},{4,5},{5,4},{6,7},{7,6},{8,9},{9,8},{10,11... | collective-permute-start | bytes 442376 | tf_op jit(solution)/shard_map/ppermute | solution.py:253
  25.1 2.6 %collective-permute-start.8 = (bf16[96,768]{1,0:T(8,128)(2,1)S(1)}, bf16[96,768]{1,0:T(8,128)(2,1)S(1)}, u32[]{:S(2)}, u32[]{:S(2)}) collective-permute-start(bf16[96,768]{1,0:T(8,128)(2,1)S(1)} %get-tuple-element.89), channel_id=1, source_target_pairs={{0,2},{1,3},{2,0},{3,1},{4,6},{5,7},{6,4},{7,5},{8,10},{9,11},{10,... | collective-permute-start | bytes 442376 | tf_op jit(solution)/shard_map/ppermute | solution.py:253
  27.9 5.2 %fetch.4 = (bf16[1536,1024]{1,0:T(8,128)(2,1)S(1)}, bf16[1536,1024]{1,0:T(8,128)(2,1)S(1)}, bf16[1536,1024]{1,0:T(8,128)(2,1)S(1)}, bf16[1536,1024]{1,0:T(8,128)(2,1)S(1)}) custom-call(s32[8]{0:T(128)S(1)} %get-tuple-element.72.at_ref, bf16[1,6144,1024]{2,1,0:T(8,128)(2,1)} %src.4, f32[96,768]{1,0:T(8,128)S(1)} %get-tuple-element.82.refs_0_), custom_call_target="tpu_custom_call" | custom-call | bytes 12582912 | tf_op jit(solution)/shard_map/fetch/pallas_call | solution.py:236
  33.2 5.9 %collective-permute-done.8 = bf16[96,768]{1,0:T(8,128)(2,1)S(1)} collective-permute-done((bf16[96,768]{1,0:T(8,128)(2,1)S(1)}, bf16[96,768]{1,0:T(8,128)(2,1)S(1)}, u32[]{:S(2)}, u32[]{:S(2)}) %collective-permute-start.8) | collective-permute-done | bytes 147488 | tf_op jit(solution)/shard_map/ppermute | solution.py:253
  39.4 2.8 %collective-permute-start.10 = (bf16[64,768]{1,0:T(8,128)(2,1)S(1)}, bf16[64,768]{1,0:T(8,128)(2,1)S(1)}, u32[]{:S(2)}, u32[]{:S(2)}) collective-permute-start(bf16[64,768]{1,0:T(8,128)(2,1)S(1)} %get-tuple-element.138), channel_id=1, source_target_pairs={{0,1},{1,0},{2,3},{3,2},{4,5},{5,4},{6,7},{7,6},{8,9},{9,8},{10,11... | collective-permute-start | bytes 294920 | tf_op jit(solution)/shard_map/ppermute | solution.py:253
  42.3 1.1 collective-permute-start.11
  43.4 1.4 %collective-permute-start.12 = (bf16[64,768]{1,0:T(8,128)(2,1)S(1)}, bf16[64,768]{1,0:T(8,128)(2,1)S(1)}, u32[]{:S(2)}, u32[]{:S(2)}) collective-permute-start(bf16[64,768]{1,0:T(8,128)(2,1)S(1)} %get-tuple-element.136), channel_id=1, source_target_pairs={{0,3},{1,2},{2,1},{3,0},{4,7},{5,6},{6,5},{7,4},{8,11},{9,10},{10,... | collective-permute-start | bytes 294920 | tf_op jit(solution)/shard_map/ppermute | solution.py:253
  44.8 1.5 %collective-permute-start.13 = (bf16[64,768]{1,0:T(8,128)(2,1)S(1)}, bf16[64,768]{1,0:T(8,128)(2,1)S(1)}, u32[]{:S(2)}, u32[]{:S(2)}) collective-permute-start(bf16[64,768]{1,0:T(8,128)(2,1)S(1)} %get-tuple-element.135), channel_id=1, source_target_pairs={{0,16},{4,20},{8,24},{12,28},{16,0},{20,4},{24,8},{28,12},{1,17},{... | collective-permute-start | bytes 294920 | tf_op jit(solution)/shard_map/ppermute | solution.py:253
  46.3 1.3 %collective-permute-start.14 = (bf16[64,768]{1,0:T(8,128)(2,1)S(1)}, bf16[64,768]{1,0:T(8,128)(2,1)S(1)}, u32[]{:S(2)}, u32[]{:S(2)}) collective-permute-start(bf16[64,768]{1,0:T(8,128)(2,1)S(1)} %get-tuple-element.135), channel_id=1, source_target_pairs={{0,24},{4,28},{8,16},{12,20},{16,8},{20,12},{24,0},{28,4},{1,25},{... | collective-permute-start | bytes 294920 | tf_op jit(solution)/shard_map/ppermute | solution.py:253
  47.6 4.4 %collective-permute-done.11 = bf16[64,768]{1,0:T(8,128)(2,1)S(1)} collective-permute-done((bf16[64,768]{1,0:T(8,128)(2,1)S(1)}, bf16[64,768]{1,0:T(8,128)(2,1)S(1)}, u32[]{:S(2)}, u32[]{:S(2)}) %collective-permute-start.11) | collective-permute-done | bytes 98336 | tf_op jit(solution)/shard_map/ppermute | solution.py:253
  52.2 1.4 %collective-permute-start.17 = (bf16[256,768]{1,0:T(8,128)(2,1)S(1)}, bf16[256,768]{1,0:T(8,128)(2,1)S(1)}, u32[]{:S(2)}, u32[]{:S(2)}) collective-permute-start(bf16[256,768]{1,0:T(8,128)(2,1)S(1)} %pad_maximum_fusion), channel_id=1, source_target_pairs={{0,8},{4,12},{8,0},{12,4},{16,24},{20,28},{24,16},{28,20},{1,9},{5... | collective-permute-start | bytes 1179656 | tf_op jit(solution)/shard_map/ppermute | solution.py:253
  53.7 1.5 %collective-permute-start.16 = (bf16[192,768]{1,0:T(8,128)(2,1)S(1)}, bf16[192,768]{1,0:T(8,128)(2,1)S(1)}, u32[]{:S(2)}, u32[]{:S(2)}) collective-permute-start(bf16[192,768]{1,0:T(8,128)(2,1)S(1)} %pad_maximum_fusion.2), channel_id=1, source_target_pairs={{0,16},{4,20},{8,24},{12,28},{16,0},{20,4},{24,8},{28,12},{1,17},{... | collective-permute-start | bytes 884744 | tf_op jit(solution)/shard_map/ppermute | solution.py:253
  55.2 0.6 collective-permute-start.15
  55.8 0.6 fusion.42
  56.4 0.6 fusion.44
  57.0 0.6 fusion.48.refs_0_
  57.6 0.6 fusion.51.refs_1_
  58.2 5.3 %fetch.5 = (bf16[1024,1536]{1,0:T(8,128)(2,1)S(1)}, bf16[1024,1536]{1,0:T(8,128)(2,1)S(1)}, bf16[1024,1536]{1,0:T(8,128)(2,1)S(1)}, bf16[1024,1536]{1,0:T(8,128)(2,1)S(1)}) custom-call(s32[8]{0:T(128)S(1)} %get-tuple-element.72.at_ref, bf16[1,1024,6144]{2,1,0:T(8,128)(2,1)} %src.5, f32[256,1024]{1,0:T(8,128)S(1)} %fusion.48.refs_0_, ...), custom_call_target="tpu_custom_call" | custom-call | bytes 12582912 | tf_op jit(solution)/shard_map/fetch/pallas_call | solution.py:236
  63.5 0.7 collective-permute-done.17
  64.2 0.6 fusion.34
  64.8 0.6 fusion.38
  65.4 0.6 collective-permute-done.19
  65.9 0.6 add_add_fusion.2
  66.5 0.6 add_add_fusion.3
  67.4 0.6 fusion.26
  67.9 0.6 fusion.30
  69.0 0.6 add_add_fusion
  69.6 0.6 add_add_fusion.1
  70.1 0.9 collective-permute-done.15
  71.1 0.6 fusion.22
  71.7 0.6 fusion.18
  72.3 0.5 collective-permute-done.21
  72.9 0.7 fusion.20
  73.6 0.8 multiply_convert_fusion
  74.4 0.6 fusion.75
  75.2 0.6 fusion.78
  76.3 0.5 collective-permute-done.22
  76.8 0.6 fusion.72
  77.6 0.6 fusion.69
  78.2 0.6 fusion.84
  79.3 0.6 fusion.81
  80.1 0.7 collective-permute-start.26
  80.8 2.2 %collective-permute-start.25 = (bf16[192,768]{1,0:T(8,128)(2,1)S(1)}, bf16[192,768]{1,0:T(8,128)(2,1)S(1)}, u32[]{:S(2)}, u32[]{:S(2)}) collective-permute-start(bf16[192,768]{1,0:T(8,128)(2,1)S(1)} %slice.172), channel_id=1, source_target_pairs={{0,24},{4,28},{8,16},{12,20},{16,8},{20,12},{24,0},{28,4},{1,25},{... | collective-permute-start | bytes 884744 | tf_op jit(solution)/shard_map/ppermute | solution.py:253
  83.0 0.6 fusion.66
  83.6 0.7 collective-permute-start.28
  84.3 0.6 fusion.60
  84.9 10.8 %collective-permute-done.26 = bf16[192,768]{1,0:T(8,128)(2,1)S(1)} collective-permute-done((bf16[192,768]{1,0:T(8,128)(2,1)S(1)}, bf16[192,768]{1,0:T(8,128)(2,1)S(1)}, u32[]{:S(2)}, u32[]{:S(2)}) %collective-permute-start.26) | collective-permute-done | bytes 294944 | tf_op jit(solution)/shard_map/ppermute | solution.py:253
  95.7 1.2 %collective-permute-done.28 = bf16[192,768]{1,0:T(8,128)(2,1)S(1)} collective-permute-done((bf16[192,768]{1,0:T(8,128)(2,1)S(1)}, bf16[192,768]{1,0:T(8,128)(2,1)S(1)}, u32[]{:S(2)}, u32[]{:S(2)}) %collective-permute-start.28) | collective-permute-done | bytes 294944 | tf_op jit(solution)/shard_map/ppermute | solution.py:253
  97.1 1.7 %collective-permute-start.29 = (bf16[64,768]{1,0:T(8,128)(2,1)S(1)}, bf16[64,768]{1,0:T(8,128)(2,1)S(1)}, u32[]{:S(2)}, u32[]{:S(2)}) collective-permute-start(bf16[64,768]{1,0:T(8,128)(2,1)S(1)} %get-tuple-element.141), channel_id=1, source_target_pairs={{0,1},{1,0},{2,3},{3,2},{4,5},{5,4},{6,7},{7,6},{8,9},{9,8},{10,11... | collective-permute-start | bytes 294920 | tf_op jit(solution)/shard_map/ppermute | solution.py:253
  98.8 1.1 collective-permute-start.30
  99.8 1.7 %collective-permute-start.31 = (bf16[64,768]{1,0:T(8,128)(2,1)S(1)}, bf16[64,768]{1,0:T(8,128)(2,1)S(1)}, u32[]{:S(2)}, u32[]{:S(2)}) collective-permute-start(bf16[64,768]{1,0:T(8,128)(2,1)S(1)} %get-tuple-element.139), channel_id=1, source_target_pairs={{0,3},{1,2},{2,1},{3,0},{4,7},{5,6},{6,5},{7,4},{8,11},{9,10},{10,... | collective-permute-start | bytes 294920 | tf_op jit(solution)/shard_map/ppermute | solution.py:253
  101.6 1.5 %collective-permute-start.32 = (bf16[64,768]{1,0:T(8,128)(2,1)S(1)}, bf16[64,768]{1,0:T(8,128)(2,1)S(1)}, u32[]{:S(2)}, u32[]{:S(2)}) collective-permute-start(bf16[64,768]{1,0:T(8,128)(2,1)S(1)} %slice.171), channel_id=1, source_target_pairs={{0,24},{4,28},{8,16},{12,20},{16,8},{20,12},{24,0},{28,4},{1,25},{... | collective-permute-start | bytes 294920 | tf_op jit(solution)/shard_map/ppermute | solution.py:253
  103.0 1.4 %collective-permute-start.33 = (bf16[64,768]{1,0:T(8,128)(2,1)S(1)}, bf16[64,768]{1,0:T(8,128)(2,1)S(1)}, u32[]{:S(2)}, u32[]{:S(2)}) collective-permute-start(bf16[64,768]{1,0:T(8,128)(2,1)S(1)} %slice.173), channel_id=1, source_target_pairs={{0,16},{4,20},{8,24},{12,28},{16,0},{20,4},{24,8},{28,12},{1,17},{... | collective-permute-start | bytes 294920 | tf_op jit(solution)/shard_map/ppermute | solution.py:253
  104.4 0.7 collective-permute-start.34
  105.1 3.5 %collective-permute-done.30 = bf16[64,768]{1,0:T(8,128)(2,1)S(1)} collective-permute-done((bf16[64,768]{1,0:T(8,128)(2,1)S(1)}, bf16[64,768]{1,0:T(8,128)(2,1)S(1)}, u32[]{:S(2)}, u32[]{:S(2)}) %collective-permute-start.30) | collective-permute-done | bytes 98336 | tf_op jit(solution)/shard_map/ppermute | solution.py:253
  109.3 0.9 add_convert_fusion
  (70 shorter events, 5.8 us)
Async XLA Ops:
  8.2 10.8 %collective-permute-start = (bf16[48,1536]{1,0:T(8,128)(2,1)S(1)}, bf16[48,1536]{1,0:T(8,128)(2,1)S(1)}, u32[]{:S(2)}, u32[]{:S(2)}) collective-permute-start(bf16[48,1536]{1,0:T(8,128)(2,1)S(1)} %get-tuple-element.77.refs_0_), channel_id=1, source_target_pairs={{0,8},{4,12},{8,0},{12,4},{16,24},{20,28},{24,16},{28,20},{1,9},{5... | collective-permute-start | bytes 442376 | tf_op jit(solution)/shard_map/ppermute | solution.py:253
  11.2 8.5 %collective-permute-start.1 = (bf16[48,1536]{1,0:T(8,128)(2,1)S(1)}, bf16[48,1536]{1,0:T(8,128)(2,1)S(1)}, u32[]{:S(2)}, u32[]{:S(2)}) collective-permute-start(bf16[48,1536]{1,0:T(8,128)(2,1)S(1)} %get-tuple-element.77.refs_0_), channel_id=1, source_target_pairs={{0,16},{4,20},{8,24},{12,28},{16,0},{20,4},{24,8},{28,12},{1,17},{... | collective-permute-start | bytes 442376 | tf_op jit(solution)/shard_map/ppermute | solution.py:253
  12.7 7.0 %collective-permute-start.2 = (bf16[48,1536]{1,0:T(8,128)(2,1)S(1)}, bf16[48,1536]{1,0:T(8,128)(2,1)S(1)}, u32[]{:S(2)}, u32[]{:S(2)}) collective-permute-start(bf16[48,1536]{1,0:T(8,128)(2,1)S(1)} %get-tuple-element.77.refs_0_), channel_id=1, source_target_pairs={{0,24},{4,28},{8,16},{12,20},{16,8},{20,12},{24,0},{28,4},{1,25},{... | collective-permute-start | bytes 442376 | tf_op jit(solution)/shard_map/ppermute | solution.py:253
  19.7 1.4 %collective-permute-start.3 = (bf16[48,1536]{1,0:T(8,128)(2,1)S(1)}, bf16[48,1536]{1,0:T(8,128)(2,1)S(1)}, u32[]{:S(2)}, u32[]{:S(2)}) collective-permute-start(bf16[48,1536]{1,0:T(8,128)(2,1)S(1)} %get-tuple-element.77.refs_0_), channel_id=1, source_target_pairs={{0,4},{4,0},{8,12},{12,8},{16,20},{20,16},{24,28},{28,24},{1,5},{5... | collective-permute-start | bytes 442376 | tf_op jit(solution)/shard_map/ppermute | solution.py:253
  19.7 1.6 %collective-permute-start.4 = (bf16[48,1536]{1,0:T(8,128)(2,1)S(1)}, bf16[48,1536]{1,0:T(8,128)(2,1)S(1)}, u32[]{:S(2)}, u32[]{:S(2)}) collective-permute-start(bf16[48,1536]{1,0:T(8,128)(2,1)S(1)} %collective-permute-done.refs_1_), channel_id=1, source_target_pairs={{0,4},{4,0},{8,12},{12,8},{16,20},{20,16},{24,28},{28,24},{1,5},{5... | collective-permute-start | bytes 442376 | tf_op jit(solution)/shard_map/ppermute | solution.py:253
  20.2 1.4 %collective-permute-start.5 = (bf16[48,1536]{1,0:T(8,128)(2,1)S(1)}, bf16[48,1536]{1,0:T(8,128)(2,1)S(1)}, u32[]{:S(2)}, u32[]{:S(2)}) collective-permute-start(bf16[48,1536]{1,0:T(8,128)(2,1)S(1)} %collective-permute-done.1.refs_2_), channel_id=1, source_target_pairs={{0,4},{4,0},{8,12},{12,8},{16,20},{20,16},{24,28},{28,24},{1,5},{5... | collective-permute-start | bytes 442376 | tf_op jit(solution)/shard_map/ppermute | solution.py:253
  20.2 1.6 %collective-permute-start.6 = (bf16[48,1536]{1,0:T(8,128)(2,1)S(1)}, bf16[48,1536]{1,0:T(8,128)(2,1)S(1)}, u32[]{:S(2)}, u32[]{:S(2)}) collective-permute-start(bf16[48,1536]{1,0:T(8,128)(2,1)S(1)} %collective-permute-done.2.refs_3_), channel_id=1, source_target_pairs={{0,4},{4,0},{8,12},{12,8},{16,20},{20,16},{24,28},{28,24},{1,5},{5... | collective-permute-start | bytes 442376 | tf_op jit(solution)/shard_map/ppermute | solution.py:253
  23.5 9.8 %collective-permute-start.7 = (bf16[96,768]{1,0:T(8,128)(2,1)S(1)}, bf16[96,768]{1,0:T(8,128)(2,1)S(1)}, u32[]{:S(2)}, u32[]{:S(2)}) collective-permute-start(bf16[96,768]{1,0:T(8,128)(2,1)S(1)} %get-tuple-element.88), channel_id=1, source_target_pairs={{0,1},{1,0},{2,3},{3,2},{4,5},{5,4},{6,7},{7,6},{8,9},{9,8},{10,11... | collective-permute-start | bytes 442376 | tf_op jit(solution)/shard_map/ppermute | solution.py:253
  25.1 14.0 %collective-permute-start.8 = (bf16[96,768]{1,0:T(8,128)(2,1)S(1)}, bf16[96,768]{1,0:T(8,128)(2,1)S(1)}, u32[]{:S(2)}, u32[]{:S(2)}) collective-permute-start(bf16[96,768]{1,0:T(8,128)(2,1)S(1)} %get-tuple-element.89), channel_id=1, source_target_pairs={{0,2},{1,3},{2,0},{3,1},{4,6},{5,7},{6,4},{7,5},{8,10},{9,11},{10,... | collective-permute-start | bytes 442376 | tf_op jit(solution)/shard_map/ppermute | solution.py:253
  27.7 11.4 %collective-permute-start.9 = (bf16[96,768]{1,0:T(8,128)(2,1)S(1)}, bf16[96,768]{1,0:T(8,128)(2,1)S(1)}, u32[]{:S(2)}, u32[]{:S(2)}) collective-permute-start(bf16[96,768]{1,0:T(8,128)(2,1)S(1)} %get-tuple-element.90), channel_id=1, source_target_pairs={{0,3},{1,2},{2,1},{3,0},{4,7},{5,6},{6,5},{7,4},{8,11},{9,10},{10,... | collective-permute-start | bytes 442376 | tf_op jit(solution)/shard_map/ppermute | solution.py:253
  27.9 5.3 %copy-start = (bf16[96,768]{1,0:T(8,128)(2,1)S(1)}, bf16[96,768]{1,0:T(8,128)(2,1)}, u32[]{:S(2)}) copy-start(bf16[96,768]{1,0:T(8,128)(2,1)} %param.13) | copy-start | bytes 442372
  39.4 8.2 %collective-permute-start.10 = (bf16[64,768]{1,0:T(8,128)(2,1)S(1)}, bf16[64,768]{1,0:T(8,128)(2,1)S(1)}, u32[]{:S(2)}, u32[]{:S(2)}) collective-permute-start(bf16[64,768]{1,0:T(8,128)(2,1)S(1)} %get-tuple-element.138), channel_id=1, source_target_pairs={{0,1},{1,0},{2,3},{3,2},{4,5},{5,4},{6,7},{7,6},{8,9},{9,8},{10,11... | collective-permute-start | bytes 294920 | tf_op jit(solution)/shard_map/ppermute | solution.py:253
  42.3 9.8 %collective-permute-start.11 = (bf16[64,768]{1,0:T(8,128)(2,1)S(1)}, bf16[64,768]{1,0:T(8,128)(2,1)S(1)}, u32[]{:S(2)}, u32[]{:S(2)}) collective-permute-start(bf16[64,768]{1,0:T(8,128)(2,1)S(1)} %get-tuple-element.137), channel_id=1, source_target_pairs={{0,2},{1,3},{2,0},{3,1},{4,6},{5,7},{6,4},{7,5},{8,10},{9,11},{10,... | collective-permute-start | bytes 294920 | tf_op jit(solution)/shard_map/ppermute | solution.py:253
  43.4 8.7 %collective-permute-start.12 = (bf16[64,768]{1,0:T(8,128)(2,1)S(1)}, bf16[64,768]{1,0:T(8,128)(2,1)S(1)}, u32[]{:S(2)}, u32[]{:S(2)}) collective-permute-start(bf16[64,768]{1,0:T(8,128)(2,1)S(1)} %get-tuple-element.136), channel_id=1, source_target_pairs={{0,3},{1,2},{2,1},{3,0},{4,7},{5,6},{6,5},{7,4},{8,11},{9,10},{10,... | collective-permute-start | bytes 294920 | tf_op jit(solution)/shard_map/ppermute | solution.py:253
  44.8 7.3 %collective-permute-start.13 = (bf16[64,768]{1,0:T(8,128)(2,1)S(1)}, bf16[64,768]{1,0:T(8,128)(2,1)S(1)}, u32[]{:S(2)}, u32[]{:S(2)}) collective-permute-start(bf16[64,768]{1,0:T(8,128)(2,1)S(1)} %get-tuple-element.135), channel_id=1, source_target_pairs={{0,16},{4,20},{8,24},{12,28},{16,0},{20,4},{24,8},{28,12},{1,17},{... | collective-permute-start | bytes 294920 | tf_op jit(solution)/shard_map/ppermute | solution.py:253
  46.3 5.8 %collective-permute-start.14 = (bf16[64,768]{1,0:T(8,128)(2,1)S(1)}, bf16[64,768]{1,0:T(8,128)(2,1)S(1)}, u32[]{:S(2)}, u32[]{:S(2)}) collective-permute-start(bf16[64,768]{1,0:T(8,128)(2,1)S(1)} %get-tuple-element.135), channel_id=1, source_target_pairs={{0,24},{4,28},{8,16},{12,20},{16,8},{20,12},{24,0},{28,4},{1,25},{... | collective-permute-start | bytes 294920 | tf_op jit(solution)/shard_map/ppermute | solution.py:253
  52.1 4.2 %collective-permute-start.18 = (bf16[256,768]{1,0:T(8,128)(2,1)S(1)}, bf16[256,768]{1,0:T(8,128)(2,1)S(1)}, u32[]{:S(2)}, u32[]{:S(2)}) collective-permute-start(bf16[256,768]{1,0:T(8,128)(2,1)S(1)} %pad_maximum_fusion), channel_id=1, source_target_pairs={{0,4},{4,0},{8,12},{12,8},{16,20},{20,16},{24,28},{28,24},{1,5},{5... | collective-permute-start | bytes 1179656 | tf_op jit(solution)/shard_map/ppermute | solution.py:253
  52.2 12.0 %collective-permute-start.17 = (bf16[256,768]{1,0:T(8,128)(2,1)S(1)}, bf16[256,768]{1,0:T(8,128)(2,1)S(1)}, u32[]{:S(2)}, u32[]{:S(2)}) collective-permute-start(bf16[256,768]{1,0:T(8,128)(2,1)S(1)} %pad_maximum_fusion), channel_id=1, source_target_pairs={{0,8},{4,12},{8,0},{12,4},{16,24},{20,28},{24,16},{28,20},{1,9},{5... | collective-permute-start | bytes 1179656 | tf_op jit(solution)/shard_map/ppermute | solution.py:253
  53.7 13.5 %collective-permute-start.16 = (bf16[192,768]{1,0:T(8,128)(2,1)S(1)}, bf16[192,768]{1,0:T(8,128)(2,1)S(1)}, u32[]{:S(2)}, u32[]{:S(2)}) collective-permute-start(bf16[192,768]{1,0:T(8,128)(2,1)S(1)} %pad_maximum_fusion.2), channel_id=1, source_target_pairs={{0,16},{4,20},{8,24},{12,28},{16,0},{20,4},{24,8},{28,12},{1,17},{... | collective-permute-start | bytes 884744 | tf_op jit(solution)/shard_map/ppermute | solution.py:253
  55.2 15.9 %collective-permute-start.15 = (bf16[192,768]{1,0:T(8,128)(2,1)S(1)}, bf16[192,768]{1,0:T(8,128)(2,1)S(1)}, u32[]{:S(2)}, u32[]{:S(2)}) collective-permute-start(bf16[192,768]{1,0:T(8,128)(2,1)S(1)} %pad_maximum_fusion.2), channel_id=1, source_target_pairs={{0,24},{4,28},{8,16},{12,20},{16,8},{20,12},{24,0},{28,4},{1,25},{... | collective-permute-start | bytes 884744 | tf_op jit(solution)/shard_map/ppermute | solution.py:253
  64.2 1.7 %collective-permute-start.19 = (bf16[256,768]{1,0:T(8,128)(2,1)S(1)}, bf16[256,768]{1,0:T(8,128)(2,1)S(1)}, u32[]{:S(2)}, u32[]{:S(2)}) collective-permute-start(bf16[256,768]{1,0:T(8,128)(2,1)S(1)} %collective-permute-done.17), channel_id=1, source_target_pairs={{0,4},{4,0},{8,12},{12,8},{16,20},{20,16},{24,28},{28,24},{1,5},{5... | collective-permute-start | bytes 1179656 | tf_op jit(solution)/shard_map/ppermute | solution.py:253
  67.2 1.8 %collective-permute-start.20 = (bf16[256,768]{1,0:T(8,128)(2,1)S(1)}, bf16[256,768]{1,0:T(8,128)(2,1)S(1)}, u32[]{:S(2)}, u32[]{:S(2)}) collective-permute-start(bf16[256,768]{1,0:T(8,128)(2,1)S(1)} %constant_dynamic-update-slice_fusion), channel_id=1, source_target_pairs={{0,4},{4,0},{8,12},{12,8},{16,20},{20,16},{24,28},{28,24},{1,5},{5... | collective-permute-start | bytes 1179656 | tf_op jit(solution)/shard_map/ppermute | solution.py:253
  71.1 1.8 %collective-permute-start.21 = (bf16[256,768]{1,0:T(8,128)(2,1)S(1)}, bf16[256,768]{1,0:T(8,128)(2,1)S(1)}, u32[]{:S(2)}, u32[]{:S(2)}) collective-permute-start(bf16[256,768]{1,0:T(8,128)(2,1)S(1)} %constant_dynamic-update-slice_fusion.2), channel_id=1, source_target_pairs={{0,4},{4,0},{8,12},{12,8},{16,20},{20,16},{24,28},{28,24},{1,5},{5... | collective-permute-start | bytes 1179656 | tf_op jit(solution)/shard_map/ppermute | solution.py:253
  75.0 1.8 %collective-permute-start.22 = (bf16[256,768]{1,0:T(8,128)(2,1)S(1)}, bf16[256,768]{1,0:T(8,128)(2,1)S(1)}, u32[]{:S(2)}, u32[]{:S(2)}) collective-permute-start(bf16[256,768]{1,0:T(8,128)(2,1)S(1)} %fusion.75), channel_id=1, source_target_pairs={{0,4},{4,0},{8,12},{12,8},{16,20},{20,16},{24,28},{28,24},{1,5},{5... | collective-permute-start | bytes 1179656 | tf_op jit(solution)/shard_map/ppermute | solution.py:253
  75.8 1.8 %collective-permute-start.23 = (bf16[256,768]{1,0:T(8,128)(2,1)S(1)}, bf16[256,768]{1,0:T(8,128)(2,1)S(1)}, u32[]{:S(2)}, u32[]{:S(2)}) collective-permute-start(bf16[256,768]{1,0:T(8,128)(2,1)S(1)} %fusion.78), channel_id=1, source_target_pairs={{0,4},{4,0},{8,12},{12,8},{16,20},{20,16},{24,28},{28,24},{1,5},{5... | collective-permute-start | bytes 1179656 | tf_op jit(solution)/shard_map/ppermute | solution.py:253
  78.9 4.1 %collective-permute-start.27 = (bf16[256,768]{1,0:T(8,128)(2,1)S(1)}, bf16[256,768]{1,0:T(8,128)(2,1)S(1)}, u32[]{:S(2)}, u32[]{:S(2)}) collective-permute-start(bf16[256,768]{1,0:T(8,128)(2,1)S(1)} %fusion.84), channel_id=1, source_target_pairs={{0,4},{4,0},{8,12},{12,8},{16,20},{20,16},{24,28},{28,24},{1,5},{5... | collective-permute-start | bytes 1179656 | tf_op jit(solution)/shard_map/ppermute | solution.py:253
  79.9 4.4 %collective-permute-start.24 = (bf16[256,768]{1,0:T(8,128)(2,1)S(1)}, bf16[256,768]{1,0:T(8,128)(2,1)S(1)}, u32[]{:S(2)}, u32[]{:S(2)}) collective-permute-start(bf16[256,768]{1,0:T(8,128)(2,1)S(1)} %fusion.81), channel_id=1, source_target_pairs={{0,4},{4,0},{8,12},{12,8},{16,20},{20,16},{24,28},{28,24},{1,5},{5... | collective-permute-start | bytes 1179656 | tf_op jit(solution)/shard_map/ppermute | solution.py:253
  80.1 15.6 %collective-permute-start.26 = (bf16[192,768]{1,0:T(8,128)(2,1)S(1)}, bf16[192,768]{1,0:T(8,128)(2,1)S(1)}, u32[]{:S(2)}, u32[]{:S(2)}) collective-permute-start(bf16[192,768]{1,0:T(8,128)(2,1)S(1)} %slice.174), channel_id=1, source_target_pairs={{0,16},{4,20},{8,24},{12,28},{16,0},{20,4},{24,8},{28,12},{1,17},{... | collective-permute-start | bytes 884744 | tf_op jit(solution)/shard_map/ppermute | solution.py:253
  80.8 14.9 %collective-permute-start.25 = (bf16[192,768]{1,0:T(8,128)(2,1)S(1)}, bf16[192,768]{1,0:T(8,128)(2,1)S(1)}, u32[]{:S(2)}, u32[]{:S(2)}) collective-permute-start(bf16[192,768]{1,0:T(8,128)(2,1)S(1)} %slice.172), channel_id=1, source_target_pairs={{0,24},{4,28},{8,16},{12,20},{16,8},{20,12},{24,0},{28,4},{1,25},{... | collective-permute-start | bytes 884744 | tf_op jit(solution)/shard_map/ppermute | solution.py:253
  83.6 21.5 %copy-start.1 = (f32[96,2]{0,1:T(2,128)S(1)}, f32[96,2]{0,1:T(2,128)}, u32[]{:S(2)}) copy-start(f32[96,2]{0,1:T(2,128)} %param.22) | copy-start | bytes 2308
  83.6 13.3 %collective-permute-start.28 = (bf16[192,768]{1,0:T(8,128)(2,1)S(1)}, bf16[192,768]{1,0:T(8,128)(2,1)S(1)}, u32[]{:S(2)}, u32[]{:S(2)}) collective-permute-start(bf16[192,768]{1,0:T(8,128)(2,1)S(1)} %slice.177), channel_id=1, source_target_pairs={{0,8},{4,12},{8,0},{12,4},{16,24},{20,28},{24,16},{28,20},{1,9},{5... | collective-permute-start | bytes 884744 | tf_op jit(solution)/shard_map/ppermute | solution.py:253
  97.1 7.3 %collective-permute-start.29 = (bf16[64,768]{1,0:T(8,128)(2,1)S(1)}, bf16[64,768]{1,0:T(8,128)(2,1)S(1)}, u32[]{:S(2)}, u32[]{:S(2)}) collective-permute-start(bf16[64,768]{1,0:T(8,128)(2,1)S(1)} %get-tuple-element.141), channel_id=1, source_target_pairs={{0,1},{1,0},{2,3},{3,2},{4,5},{5,4},{6,7},{7,6},{8,9},{9,8},{10,11... | collective-permute-start | bytes 294920 | tf_op jit(solution)/shard_map/ppermute | solution.py:253
  98.8 9.8 %collective-permute-start.30 = (bf16[64,768]{1,0:T(8,128)(2,1)S(1)}, bf16[64,768]{1,0:T(8,128)(2,1)S(1)}, u32[]{:S(2)}, u32[]{:S(2)}) collective-permute-start(bf16[64,768]{1,0:T(8,128)(2,1)S(1)} %get-tuple-element.140), channel_id=1, source_target_pairs={{0,2},{1,3},{2,0},{3,1},{4,6},{5,7},{6,4},{7,5},{8,10},{9,11},{10,... | collective-permute-start | bytes 294920 | tf_op jit(solution)/shard_map/ppermute | solution.py:253
  99.8 8.8 %collective-permute-start.31 = (bf16[64,768]{1,0:T(8,128)(2,1)S(1)}, bf16[64,768]{1,0:T(8,128)(2,1)S(1)}, u32[]{:S(2)}, u32[]{:S(2)}) collective-permute-start(bf16[64,768]{1,0:T(8,128)(2,1)S(1)} %get-tuple-element.139), channel_id=1, source_target_pairs={{0,3},{1,2},{2,1},{3,0},{4,7},{5,6},{6,5},{7,4},{8,11},{9,10},{10,... | collective-permute-start | bytes 294920 | tf_op jit(solution)/shard_map/ppermute | solution.py:253
  101.6 7.0 %collective-permute-start.32 = (bf16[64,768]{1,0:T(8,128)(2,1)S(1)}, bf16[64,768]{1,0:T(8,128)(2,1)S(1)}, u32[]{:S(2)}, u32[]{:S(2)}) collective-permute-start(bf16[64,768]{1,0:T(8,128)(2,1)S(1)} %slice.171), channel_id=1, source_target_pairs={{0,24},{4,28},{8,16},{12,20},{16,8},{20,12},{24,0},{28,4},{1,25},{... | collective-permute-start | bytes 294920 | tf_op jit(solution)/shard_map/ppermute | solution.py:253
  103.0 5.6 %collective-permute-start.33 = (bf16[64,768]{1,0:T(8,128)(2,1)S(1)}, bf16[64,768]{1,0:T(8,128)(2,1)S(1)}, u32[]{:S(2)}, u32[]{:S(2)}) collective-permute-start(bf16[64,768]{1,0:T(8,128)(2,1)S(1)} %slice.173), channel_id=1, source_target_pairs={{0,16},{4,20},{8,24},{12,28},{16,0},{20,4},{24,8},{28,12},{1,17},{... | collective-permute-start | bytes 294920 | tf_op jit(solution)/shard_map/ppermute | solution.py:253
  104.4 4.6 %collective-permute-start.34 = (bf16[64,768]{1,0:T(8,128)(2,1)S(1)}, bf16[64,768]{1,0:T(8,128)(2,1)S(1)}, u32[]{:S(2)}, u32[]{:S(2)}) collective-permute-start(bf16[64,768]{1,0:T(8,128)(2,1)S(1)} %slice.178), channel_id=1, source_target_pairs={{0,8},{4,12},{8,0},{12,4},{16,24},{20,28},{24,16},{28,20},{1,9},{5... | collective-permute-start | bytes 294920 | tf_op jit(solution)/shard_map/ppermute | solution.py:253

commit v2 on v1

--- a/solution.py
+++ b/solution.py
@@ -29,7 +29,9 @@
 def attend_kernel(
     drafts, len_hbm, q_hbm, nk_hbm, nv_hbm, ck_hbm, cv_hbm, w_hbm, o_ref, w_ref, *scratch
 ):
-    len_ref, q_ref, nk_ref, nv_ref, ck_ref, cv_ref, qs, scores, acc, sem, k_sem, v_sem, w_sem = scratch
+    len_ref, q_ref, nk_ref, nv_ref, ck_ref, cv_ref, *scratch = scratch
+    qs, spread_q, scores, new_scores, new_probs, mixed, inverse, acc, *scratch = scratch
+    sem, k_sem, v_sem, w_sem = scratch
     requests, size, width = ck_ref.shape
     rows = q_ref.shape[0]
     heads = width // HD
@@ -64,11 +66,8 @@
         copy.wait()
     qs[...] = dot(spread(rows, drafts, False), q_ref[...])
 
-    at = lax.broadcasted_iota(jnp.int32, (wide, rows), 1)
-    draft_at = lax.broadcasted_iota(jnp.int32, (wide, rows), 0) & 7
-    past_at = lax.broadcasted_iota(jnp.int32, (wide, size), 1)
-
-    def queries(r):
+    place = lax.broadcasted_iota(jnp.int32, (1, size), 1)
+    for r in range(requests):
         q_all = qs[r * 8 : (r + 1) * 8, :]
         zero = jnp.zeros((group, HD), jnp.float32)
         parts = []
@@ -81,34 +80,33 @@
                 axis=0,
             )
             parts.append(jnp.concatenate([q if j == h else zero for j in range(heads)], axis=1))
-        return jnp.concatenate(parts, axis=0).astype(jnp.bfloat16)
+        spread_q[r * wide : (r + 1) * wide, :] = jnp.concatenate(parts, axis=0).astype(jnp.bfloat16)
+    new_scores[...] = lax.dot_general(
+        spread_q[...], nk_ref[...], NT, preferred_element_type=jnp.float32
+    )
+    at = lax.broadcasted_iota(jnp.int32, (wide, rows), 1)
+    draft_at = lax.broadcasted_iota(jnp.int32, (wide, rows), 0) & 7
 
     def score(r):
-        past = lax.dot_general(queries(r), ck_ref[r], NT, preferred_element_type=jnp.float32)
-        scores[r % 4] = jnp.where(past_at < len_ref[r], past * SCALE, MASKED)
+        here = slice(r * wide, (r + 1) * wide)
+        past = lax.dot_general(spread_q[here, :], ck_ref[r], NT, preferred_element_type=jnp.float32)
+        scores[r % 4] = past * SCALE + jnp.where(place < len_ref[r], 0.0, MASKED)
 
     def mix(r):
+        here = slice(r * wide, (r + 1) * wide)
         past = scores[r % 4]
-        new = lax.dot_general(queries(r), nk_ref[...], NT, preferred_element_type=jnp.float32)
         key_at = at - r * drafts
         new_ok = (key_at >= 0) & (key_at <= draft_at) & (key_at < drafts)
-        new = jnp.where(new_ok, new * SCALE, MASKED)
+        new = jnp.where(new_ok, new_scores[here, :] * SCALE, MASKED)
         top = jnp.maximum(
             jnp.max(past, axis=1, keepdims=True), jnp.max(new, axis=1, keepdims=True)
         )
         past = jnp.exp(past - top)
         new = jnp.exp(new - top)
         total = jnp.sum(past, axis=1, keepdims=True) + jnp.sum(new, axis=1, keepdims=True)
-        inverse = 1.0 / total
-        mixed = dot((past * inverse).astype(jnp.bfloat16), cv_ref[r])
-        mixed = mixed + dot((new * inverse).astype(jnp.bfloat16), nv_ref[...])
-        for h in range(heads):
-            for g in range(GROUPS):
-                col = (h * GROUPS + g) * HD
-                row = h * group + g * 8
-                acc[r * 8 : (r + 1) * 8, col : col + HD] = mixed[
-                    row : row + 8, h * HD : (h + 1) * HD
-                ]
+        inverse[here, :] = jnp.broadcast_to(1.0 / total, (wide, HD))
+        new_probs[here, :] = new.astype(jnp.bfloat16)
+        mixed[here, :] = dot(past.astype(jnp.bfloat16), cv_ref[r])
 
     pairs = [range(i, min(i + 2, requests)) for i in range(0, requests, 2)]
     for r in pairs[0]:
@@ -125,6 +123,15 @@
             score(r)
         for r in pair:
             mix(r)
+    mixed[...] = mixed[...] + dot(new_probs[...], nv_ref[...])
+    for r in range(requests):
+        for h in range(heads):
+            for g in range(GROUPS):
+                col = (h * GROUPS + g) * HD
+                row = slice(r * wide + h * group + g * 8, r * wide + h * group + (g + 1) * 8)
+                acc[r * 8 : (r + 1) * 8, col : col + HD] = (
+                    mixed[row, h * HD : (h + 1) * HD] * inverse[row, :]
+                )
     kept = spread(rows, drafts, True)
     o_ref[...] = dot(kept, acc[...].astype(jnp.bfloat16)).astype(jnp.bfloat16)
     for copy in weights:
@@ -156,7 +163,12 @@
             pltpu.VMEM(cache_keys.shape, bf16),
             pltpu.VMEM(cache_values.shape, bf16),
             pltpu.VMEM((requests * 8, q_width), f32),
+            pltpu.VMEM((requests * wide, width), bf16),
             pltpu.VMEM((4, wide, size), f32),
+            pltpu.VMEM((requests * wide, rows), f32),
+            pltpu.VMEM((requests * wide, rows), bf16),
+            pltpu.VMEM((requests * wide, width), f32),
+            pltpu.VMEM((requests * wide, HD), f32),
             pltpu.VMEM((requests * 8, q_width), f32),
             pltpu.SemaphoreType.DMA((4,)),
             pltpu.SemaphoreType.DMA((requests,)),
@@ -334,25 +346,20 @@
         pick, hidden_in, (((0,), (0,)), ((), ())), preferred_element_type=f32
     ).astype(bf16)
     buffers = buffers.reshape(experts, slots, width)
-    early = [k for k in range(1, chips) if k & 2]
-    first = {k: swap(buffers[0], "section", 2 * k) for k in early}
+    first = {k: swap(buffers[0], "section", 2 * k) for k in range(1, chips)}
     rest = jnp.concatenate(exchange(buffers), axis=0)
     rest, first = lax.optimization_barrier((rest, first))
+    down_parts = fetch(w_down, 1, found, rest)
     received = jnp.concatenate([buffers[0], rest], axis=0)
-    second = {k: swap(rest if k in first else received, "section", 2 * k) for k in range(1, chips)}
+    second = {k: swap(rest, "section", 2 * k) for k in range(1, chips)}
 
     sums = []
     for k in range(chips):
-        if not k:
-            same = received
-        elif k in first:
-            first[k], second[k], sums = lax.optimization_barrier((first[k], second[k], sums))
-            same = jnp.concatenate([first[k], second[k]], axis=0)
-        elif k == 1:
-            down_parts = fetch(w_down, 1, found, *sums)
-            same, sums, down_parts = lax.optimization_barrier((second[k], sums, down_parts))
-        else:
-            same, sums = lax.optimization_barrier((second[k], sums))
+        if k:
+            first[k], second[k], down_parts, sums = lax.optimization_barrier(
+                (first[k], second[k], down_parts, sums)
+            )
+        same = jnp.concatenate([first[k], second[k]], axis=0) if k else received
         for side, piece in enumerate((same, swap(same, "section", 1))):
             here = slice(side * width, (side + 1) * width)
             parts = [dot(piece, w[k][here]) for w in (gate_parts, up_parts)]
@@ -365,7 +372,7 @@
         return dot(activated, down_parts[k][:, here])
 
     order = sorted(range(1, chips), key=lambda k: (-(k & 2), -k))
-    ahead = {k: down(k, 1).astype(bf16) for k in early}
+    ahead = {k: down(k, 1).astype(bf16) for k in order if k & 2}
     later, rest = {}, {}
     for k in order:
         for_core = ahead[k] if k in ahead else down(k, 1).astype(bf16)

time: 110 us -> 111 us (level)
    ppermute x35 -> x36, starting transfers between devices: 34.9 us -> 35.6 us  [swap(): return lax.ppermute(value, axis, [(i, i ^ mask) for i in range(size)])]
    ppermute x35 -> x36, waiting for transfers between devices: 31.7 us -> 32.4 us  [swap(): return lax.ppermute(value, axis, [(i, i ^ mask) for i in range(size)])]
  transfers between devices with their start and end apart: 35 -> 36, of which waited for: 18 -> 18; matrix products, arithmetic and copies ran while one was open for 11% -> 11% of each run, Pallas kernels for 14% -> 14%
where the time goes in v2:
time: 111 us
  starting transfers between devices  35.6 us (32%)
  waiting for transfers between devices  32.4 us (29%)
  Pallas kernels  24.7 us (22%)
  matrix products  15.8 us (14%)
  other arithmetic  1.24 us (1%)
    ppermute x36, starting transfers between devices, swap(): return lax.ppermute(value, axis, [(i, i ^ mask) for i in range(size)])  35.6 us
    ppermute x36, waiting for transfers between devices, swap(): return lax.ppermute(value, axis, [(i, i ^ mask) for i in range(size)])  32.4 us
    pallas_call x3, Pallas kernels, fetch(): pl.pallas_call(functools.partial(fetch_kernel, dim, count), in_specs=[pl....  15.8 us
    dot_general x27, matrix products, dot(): return jnp.dot(a, b, preferred_element_type=jnp.float32)  15.5 us
    pallas_call x1, Pallas kernels, attend(): pl.pallas_call(functools.partial(attend_kernel, rows // requests), in_spe...  7.26 us
  transfers between devices with their start and end apart: 36, of which 18 were waited for; matrix products, arithmetic and copies ran while one was open for 11% of the time, Pallas kernels for 14%

profile of v2, /device:TPU:0, one launch (start us, length us, event | category | flops | bytes accessed | tf_op | source)
XLA Modules:
  0.0 110.6 jit_solution(6639301766272958897)
XLA Ops:
  0.0 7.3 %attend.1 = (bf16[48,1536]{1,0:T(8,128)(2,1)S(1)}, bf16[1536,768]{1,0:T(8,128)(2,1)S(1)}) custom-call(s32[8]{0:T(128)} %len_hbm.1, bf16[48,1536]{1,0:T(8,128)(2,1)} %q_hbm.1, bf16[48,256]{1,0:T(8,128)(2,1)} %nk_hbm.1, bf16[48,256]{1,0:T(8,128)(2,1)} %nv_hbm.1, bf16[8,1024,256]{2,1,0:T(8,128)(2,1)} %ck_hbm.1, bf16[8,1024,256]{2,1,0:T(8,128)(2,1)} %cv_hbm.1, ...), custom_call_target="tpu_custom_call" | custom-call | flops 301989888 | bytes 8388608 | tf_op jit(solution)/shard_map/attend/pallas_call | solution.py:150
  7.3 3.0 %collective-permute-start = (bf16[48,1536]{1,0:T(8,128)(2,1)S(1)}, bf16[48,1536]{1,0:T(8,128)(2,1)S(1)}, u32[]{:S(2)}, u32[]{:S(2)}) collective-permute-start(bf16[48,1536]{1,0:T(8,128)(2,1)S(1)} %get-tuple-element.87.refs_0_), channel_id=1, source_target_pairs={{0,8},{4,12},{8,0},{12,4},{16,24},{20,28},{24,16},{28,20},{1,9},{5... | collective-permute-start | bytes 442376 | tf_op jit(solution)/shard_map/ppermute | solution.py:265
  10.3 1.5 %collective-permute-start.1 = (bf16[48,1536]{1,0:T(8,128)(2,1)S(1)}, bf16[48,1536]{1,0:T(8,128)(2,1)S(1)}, u32[]{:S(2)}, u32[]{:S(2)}) collective-permute-start(bf16[48,1536]{1,0:T(8,128)(2,1)S(1)} %get-tuple-element.87.refs_0_), channel_id=1, source_target_pairs={{0,16},{4,20},{8,24},{12,28},{16,0},{20,4},{24,8},{28,12},{1,17},{... | collective-permute-start | bytes 442376 | tf_op jit(solution)/shard_map/ppermute | solution.py:265
  11.8 0.8 dynamic-slice_xor_fusion
  12.7 5.2 %fetch.3 = (bf16[1536,1024]{1,0:T(8,128)(2,1)S(1)}, bf16[1536,1024]{1,0:T(8,128)(2,1)S(1)}, bf16[1536,1024]{1,0:T(8,128)(2,1)S(1)}, bf16[1536,1024]{1,0:T(8,128)(2,1)S(1)}) custom-call(s32[8]{0:T(128)S(1)} %get-tuple-element.82.at_ref, bf16[1,6144,1024]{2,1,0:T(8,128)(2,1)} %src.3, bf16[48,1536]{1,0:T(8,128)(2,1)S(1)} %get-tuple-element.87.refs_0_), custom_call_target="tpu_custom_call" | custom-call | bytes 12582912 | tf_op jit(solution)/shard_map/fetch/pallas_call | solution.py:248
  18.1 0.7 collective-permute-done.1.refs_2_
  20.8 1.7 %project.1 = (f32[96,768]{1,0:T(8,128)S(1)}, bf16[96,768]{1,0:T(8,128)(2,1)S(1)}, bf16[96,768]{1,0:T(8,128)(2,1)S(1)}, bf16[96,768]{1,0:T(8,128)(2,1)S(1)}) custom-call(s32[8]{0:T(128)S(1)} %get-tuple-element.80.at_ref, bf16[48,1536]{1,0:T(8,128)(2,1)S(1)} %get-tuple-element.87.refs_0_, bf16[48,1536]{1,0:T(8,128)(2,1)S(1)} %collective-permute-done.refs_1_, ...), custom_call_target="tpu_custom_call" | custom-call | flops 905969664 | bytes 2359296 | tf_op jit(solution)/shard_map/project/pallas_call | solution.py:207
  22.5 1.6 %collective-permute-start.7 = (bf16[96,768]{1,0:T(8,128)(2,1)S(1)}, bf16[96,768]{1,0:T(8,128)(2,1)S(1)}, u32[]{:S(2)}, u32[]{:S(2)}) collective-permute-start(bf16[96,768]{1,0:T(8,128)(2,1)S(1)} %get-tuple-element.98), channel_id=1, source_target_pairs={{0,1},{1,0},{2,3},{3,2},{4,5},{5,4},{6,7},{7,6},{8,9},{9,8},{10,11... | collective-permute-start | bytes 442376 | tf_op jit(solution)/shard_map/ppermute | solution.py:265
  24.2 2.6 %collective-permute-start.8 = (bf16[96,768]{1,0:T(8,128)(2,1)S(1)}, bf16[96,768]{1,0:T(8,128)(2,1)S(1)}, u32[]{:S(2)}, u32[]{:S(2)}) collective-permute-start(bf16[96,768]{1,0:T(8,128)(2,1)S(1)} %get-tuple-element.99), channel_id=1, source_target_pairs={{0,2},{1,3},{2,0},{3,1},{4,6},{5,7},{6,4},{7,5},{8,10},{9,11},{10,... | collective-permute-start | bytes 442376 | tf_op jit(solution)/shard_map/ppermute | solution.py:265
  27.0 5.2 %fetch.4 = (bf16[1536,1024]{1,0:T(8,128)(2,1)S(1)}, bf16[1536,1024]{1,0:T(8,128)(2,1)S(1)}, bf16[1536,1024]{1,0:T(8,128)(2,1)S(1)}, bf16[1536,1024]{1,0:T(8,128)(2,1)S(1)}) custom-call(s32[8]{0:T(128)S(1)} %get-tuple-element.82.at_ref, bf16[1,6144,1024]{2,1,0:T(8,128)(2,1)} %src.4, f32[96,768]{1,0:T(8,128)S(1)} %get-tuple-element.92.refs_0_), custom_call_target="tpu_custom_call" | custom-call | bytes 12582912 | tf_op jit(solution)/shard_map/fetch/pallas_call | solution.py:248
  32.3 5.9 %collective-permute-done.8 = bf16[96,768]{1,0:T(8,128)(2,1)S(1)} collective-permute-done((bf16[96,768]{1,0:T(8,128)(2,1)S(1)}, bf16[96,768]{1,0:T(8,128)(2,1)S(1)}, u32[]{:S(2)}, u32[]{:S(2)}) %collective-permute-start.8) | collective-permute-done | bytes 147488 | tf_op jit(solution)/shard_map/ppermute | solution.py:265
  38.5 2.8 %collective-permute-start.10 = (bf16[64,768]{1,0:T(8,128)(2,1)S(1)}, bf16[64,768]{1,0:T(8,128)(2,1)S(1)}, u32[]{:S(2)}, u32[]{:S(2)}) collective-permute-start(bf16[64,768]{1,0:T(8,128)(2,1)S(1)} %get-tuple-element.158), channel_id=1, source_target_pairs={{0,1},{1,0},{2,3},{3,2},{4,5},{5,4},{6,7},{7,6},{8,9},{9,8},{10,11... | collective-permute-start | bytes 294920 | tf_op jit(solution)/shard_map/ppermute | solution.py:265
  41.3 1.1 collective-permute-start.11
  42.4 1.4 %collective-permute-start.12 = (bf16[64,768]{1,0:T(8,128)(2,1)S(1)}, bf16[64,768]{1,0:T(8,128)(2,1)S(1)}, u32[]{:S(2)}, u32[]{:S(2)}) collective-permute-start(bf16[64,768]{1,0:T(8,128)(2,1)S(1)} %get-tuple-element.156), channel_id=1, source_target_pairs={{0,3},{1,2},{2,1},{3,0},{4,7},{5,6},{6,5},{7,4},{8,11},{9,10},{10,... | collective-permute-start | bytes 294920 | tf_op jit(solution)/shard_map/ppermute | solution.py:265
  43.8 1.4 %collective-permute-start.13 = (bf16[64,768]{1,0:T(8,128)(2,1)S(1)}, bf16[64,768]{1,0:T(8,128)(2,1)S(1)}, u32[]{:S(2)}, u32[]{:S(2)}) collective-permute-start(bf16[64,768]{1,0:T(8,128)(2,1)S(1)} %get-tuple-element.155), channel_id=1, source_target_pairs={{0,8},{4,12},{8,0},{12,4},{16,24},{20,28},{24,16},{28,20},{1,9},{5... | collective-permute-start | bytes 294920 | tf_op jit(solution)/shard_map/ppermute | solution.py:265
  45.2 1.5 %collective-permute-start.14 = (bf16[64,768]{1,0:T(8,128)(2,1)S(1)}, bf16[64,768]{1,0:T(8,128)(2,1)S(1)}, u32[]{:S(2)}, u32[]{:S(2)}) collective-permute-start(bf16[64,768]{1,0:T(8,128)(2,1)S(1)} %get-tuple-element.155), channel_id=1, source_target_pairs={{0,16},{4,20},{8,24},{12,28},{16,0},{20,4},{24,8},{28,12},{1,17},{... | collective-permute-start | bytes 294920 | tf_op jit(solution)/shard_map/ppermute | solution.py:265
  46.7 0.6 collective-permute-start.15
  47.3 3.8 %collective-permute-done.11 = bf16[64,768]{1,0:T(8,128)(2,1)S(1)} collective-permute-done((bf16[64,768]{1,0:T(8,128)(2,1)S(1)}, bf16[64,768]{1,0:T(8,128)(2,1)S(1)}, u32[]{:S(2)}, u32[]{:S(2)}) %collective-permute-start.11) | collective-permute-done | bytes 98336 | tf_op jit(solution)/shard_map/ppermute | solution.py:265
  51.1 1.1 collective-permute-done.15
  52.3 0.7 collective-permute-start.18
  53.1 1.2 %collective-permute-start.17 = (bf16[192,768]{1,0:T(8,128)(2,1)S(1)}, bf16[192,768]{1,0:T(8,128)(2,1)S(1)}, u32[]{:S(2)}, u32[]{:S(2)}) collective-permute-start(bf16[192,768]{1,0:T(8,128)(2,1)S(1)} %pad_maximum_fusion.2.refs_0_), channel_id=1, source_target_pairs={{0,16},{4,20},{8,24},{12,28},{16,0},{20,4},{24,8},{28,12},{1,17},{... | collective-permute-start | bytes 884744 | tf_op jit(solution)/shard_map/ppermute | solution.py:265
  54.2 1.7 %collective-permute-start.16 = (bf16[192,768]{1,0:T(8,128)(2,1)S(1)}, bf16[192,768]{1,0:T(8,128)(2,1)S(1)}, u32[]{:S(2)}, u32[]{:S(2)}) collective-permute-start(bf16[192,768]{1,0:T(8,128)(2,1)S(1)} %pad_maximum_fusion.2.refs_0_), channel_id=1, source_target_pairs={{0,24},{4,28},{8,16},{12,20},{16,8},{20,12},{24,0},{28,4},{1,25},{... | collective-permute-start | bytes 884744 | tf_op jit(solution)/shard_map/ppermute | solution.py:265
  55.9 5.3 %fetch.5 = (bf16[1024,1536]{1,0:T(8,128)(2,1)S(1)}, bf16[1024,1536]{1,0:T(8,128)(2,1)S(1)}, bf16[1024,1536]{1,0:T(8,128)(2,1)S(1)}, bf16[1024,1536]{1,0:T(8,128)(2,1)S(1)}) custom-call(s32[8]{0:T(128)S(1)} %get-tuple-element.82.at_ref, bf16[1,1024,6144]{2,1,0:T(8,128)(2,1)} %src.5, bf16[192,768]{1,0:T(8,128)(2,1)S(1)} %pad_maximum_fusion.2.refs_0_), custom_call_target="tpu_custom_call" | custom-call | bytes 12582912 | tf_op jit(solution)/shard_map/fetch/pallas_call | solution.py:248
  61.2 0.6 fusion.42
  61.8 0.6 fusion.51
  62.4 0.6 fusion.44
  63.0 0.6 fusion.48
  63.7 0.6 fusion.34
  64.3 0.6 fusion.38
  64.9 0.6 collective-permute-done.20
  65.5 0.6 add_add_fusion.2
  66.0 0.6 add_add_fusion.3
  66.6 1.8 %collective-permute-done.17 = bf16[192,768]{1,0:T(8,128)(2,1)S(1)} collective-permute-done((bf16[192,768]{1,0:T(8,128)(2,1)S(1)}, bf16[192,768]{1,0:T(8,128)(2,1)S(1)}, u32[]{:S(2)}, u32[]{:S(2)}) %collective-permute-start.17) | collective-permute-done | bytes 294944 | tf_op jit(solution)/shard_map/ppermute | solution.py:265
  68.6 0.6 fusion.26
  69.2 0.6 fusion.30
  69.7 0.6 collective-permute-done.21
  70.3 0.6 add_add_fusion
  70.9 0.6 add_add_fusion.1
  71.7 0.6 fusion.22
  72.3 0.6 fusion.18
  73.3 0.6 fusion.20
  73.9 1.0 multiply_convert_fusion
  74.9 0.6 fusion.75
  75.6 0.6 fusion.78
  76.7 0.6 collective-permute-done.23
  77.2 0.6 fusion.72
  78.0 0.6 fusion.69
  78.6 0.6 fusion.84
  79.7 0.6 fusion.81
  80.4 2.8 %collective-permute-start.26 = (bf16[192,768]{1,0:T(8,128)(2,1)S(1)}, bf16[192,768]{1,0:T(8,128)(2,1)S(1)}, u32[]{:S(2)}, u32[]{:S(2)}) collective-permute-start(bf16[192,768]{1,0:T(8,128)(2,1)S(1)} %slice.173), channel_id=1, source_target_pairs={{0,24},{4,28},{8,16},{12,20},{16,8},{20,12},{24,0},{28,4},{1,25},{... | collective-permute-start | bytes 884744 | tf_op jit(solution)/shard_map/ppermute | solution.py:265
  83.3 0.6 fusion.66
  83.9 0.7 collective-permute-start.29
  84.7 0.6 fusion.60
  85.2 10.8 %collective-permute-done.27 = bf16[192,768]{1,0:T(8,128)(2,1)S(1)} collective-permute-done((bf16[192,768]{1,0:T(8,128)(2,1)S(1)}, bf16[192,768]{1,0:T(8,128)(2,1)S(1)}, u32[]{:S(2)}, u32[]{:S(2)}) %collective-permute-start.27) | collective-permute-done | bytes 294944 | tf_op jit(solution)/shard_map/ppermute | solution.py:265
  96.1 1.2 %collective-permute-done.29 = bf16[192,768]{1,0:T(8,128)(2,1)S(1)} collective-permute-done((bf16[192,768]{1,0:T(8,128)(2,1)S(1)}, bf16[192,768]{1,0:T(8,128)(2,1)S(1)}, u32[]{:S(2)}, u32[]{:S(2)}) %collective-permute-start.29) | collective-permute-done | bytes 294944 | tf_op jit(solution)/shard_map/ppermute | solution.py:265
  97.5 1.3 %collective-permute-start.30 = (bf16[64,768]{1,0:T(8,128)(2,1)S(1)}, bf16[64,768]{1,0:T(8,128)(2,1)S(1)}, u32[]{:S(2)}, u32[]{:S(2)}) collective-permute-start(bf16[64,768]{1,0:T(8,128)(2,1)S(1)} %get-tuple-element.161), channel_id=1, source_target_pairs={{0,1},{1,0},{2,3},{3,2},{4,5},{5,4},{6,7},{7,6},{8,9},{9,8},{10,11... | collective-permute-start | bytes 294920 | tf_op jit(solution)/shard_map/ppermute | solution.py:265
  98.8 1.7 %collective-permute-start.31 = (bf16[64,768]{1,0:T(8,128)(2,1)S(1)}, bf16[64,768]{1,0:T(8,128)(2,1)S(1)}, u32[]{:S(2)}, u32[]{:S(2)}) collective-permute-start(bf16[64,768]{1,0:T(8,128)(2,1)S(1)} %get-tuple-element.160), channel_id=1, source_target_pairs={{0,2},{1,3},{2,0},{3,1},{4,6},{5,7},{6,4},{7,5},{8,10},{9,11},{10,... | collective-permute-start | bytes 294920 | tf_op jit(solution)/shard_map/ppermute | solution.py:265
  100.5 1.4 %collective-permute-start.32 = (bf16[64,768]{1,0:T(8,128)(2,1)S(1)}, bf16[64,768]{1,0:T(8,128)(2,1)S(1)}, u32[]{:S(2)}, u32[]{:S(2)}) collective-permute-start(bf16[64,768]{1,0:T(8,128)(2,1)S(1)} %get-tuple-element.159), channel_id=1, source_target_pairs={{0,3},{1,2},{2,1},{3,0},{4,7},{5,6},{6,5},{7,4},{8,11},{9,10},{10,... | collective-permute-start | bytes 294920 | tf_op jit(solution)/shard_map/ppermute | solution.py:265
  101.9 1.3 %collective-permute-start.33 = (bf16[64,768]{1,0:T(8,128)(2,1)S(1)}, bf16[64,768]{1,0:T(8,128)(2,1)S(1)}, u32[]{:S(2)}, u32[]{:S(2)}) collective-permute-start(bf16[64,768]{1,0:T(8,128)(2,1)S(1)} %slice.172), channel_id=1, source_target_pairs={{0,24},{4,28},{8,16},{12,20},{16,8},{20,12},{24,0},{28,4},{1,25},{... | collective-permute-start | bytes 294920 | tf_op jit(solution)/shard_map/ppermute | solution.py:265
  103.2 1.5 %collective-permute-start.34 = (bf16[64,768]{1,0:T(8,128)(2,1)S(1)}, bf16[64,768]{1,0:T(8,128)(2,1)S(1)}, u32[]{:S(2)}, u32[]{:S(2)}) collective-permute-start(bf16[64,768]{1,0:T(8,128)(2,1)S(1)} %slice.174), channel_id=1, source_target_pairs={{0,16},{4,20},{8,24},{12,28},{16,0},{20,4},{24,8},{28,12},{1,17},{... | collective-permute-start | bytes 294920 | tf_op jit(solution)/shard_map/ppermute | solution.py:265
  104.7 0.7 collective-permute-start.35
  105.4 3.2 %collective-permute-done.31 = bf16[64,768]{1,0:T(8,128)(2,1)S(1)} collective-permute-done((bf16[64,768]{1,0:T(8,128)(2,1)S(1)}, bf16[64,768]{1,0:T(8,128)(2,1)S(1)}, u32[]{:S(2)}, u32[]{:S(2)}) %collective-permute-start.31) | collective-permute-done | bytes 98336 | tf_op jit(solution)/shard_map/ppermute | solution.py:265
  108.6 0.8 collective-permute-done.35
  109.7 0.9 add_convert_fusion
  (74 shorter events, 6.0 us)
Async XLA Ops:
  7.3 10.8 %collective-permute-start = (bf16[48,1536]{1,0:T(8,128)(2,1)S(1)}, bf16[48,1536]{1,0:T(8,128)(2,1)S(1)}, u32[]{:S(2)}, u32[]{:S(2)}) collective-permute-start(bf16[48,1536]{1,0:T(8,128)(2,1)S(1)} %get-tuple-element.87.refs_0_), channel_id=1, source_target_pairs={{0,8},{4,12},{8,0},{12,4},{16,24},{20,28},{24,16},{28,20},{1,9},{5... | collective-permute-start | bytes 442376 | tf_op jit(solution)/shard_map/ppermute | solution.py:265
  10.3 8.5 %collective-permute-start.1 = (bf16[48,1536]{1,0:T(8,128)(2,1)S(1)}, bf16[48,1536]{1,0:T(8,128)(2,1)S(1)}, u32[]{:S(2)}, u32[]{:S(2)}) collective-permute-start(bf16[48,1536]{1,0:T(8,128)(2,1)S(1)} %get-tuple-element.87.refs_0_), channel_id=1, source_target_pairs={{0,16},{4,20},{8,24},{12,28},{16,0},{20,4},{24,8},{28,12},{1,17},{... | collective-permute-start | bytes 442376 | tf_op jit(solution)/shard_map/ppermute | solution.py:265
  11.8 6.9 %collective-permute-start.2 = (bf16[48,1536]{1,0:T(8,128)(2,1)S(1)}, bf16[48,1536]{1,0:T(8,128)(2,1)S(1)}, u32[]{:S(2)}, u32[]{:S(2)}) collective-permute-start(bf16[48,1536]{1,0:T(8,128)(2,1)S(1)} %get-tuple-element.87.refs_0_), channel_id=1, source_target_pairs={{0,24},{4,28},{8,16},{12,20},{16,8},{20,12},{24,0},{28,4},{1,25},{... | collective-permute-start | bytes 442376 | tf_op jit(solution)/shard_map/ppermute | solution.py:265
  18.7 1.4 %collective-permute-start.3 = (bf16[48,1536]{1,0:T(8,128)(2,1)S(1)}, bf16[48,1536]{1,0:T(8,128)(2,1)S(1)}, u32[]{:S(2)}, u32[]{:S(2)}) collective-permute-start(bf16[48,1536]{1,0:T(8,128)(2,1)S(1)} %get-tuple-element.87.refs_0_), channel_id=1, source_target_pairs={{0,4},{4,0},{8,12},{12,8},{16,20},{20,16},{24,28},{28,24},{1,5},{5... | collective-permute-start | bytes 442376 | tf_op jit(solution)/shard_map/ppermute | solution.py:265
  18.7 1.6 %collective-permute-start.4 = (bf16[48,1536]{1,0:T(8,128)(2,1)S(1)}, bf16[48,1536]{1,0:T(8,128)(2,1)S(1)}, u32[]{:S(2)}, u32[]{:S(2)}) collective-permute-start(bf16[48,1536]{1,0:T(8,128)(2,1)S(1)} %collective-permute-done.refs_1_), channel_id=1, source_target_pairs={{0,4},{4,0},{8,12},{12,8},{16,20},{20,16},{24,28},{28,24},{1,5},{5... | collective-permute-start | bytes 442376 | tf_op jit(solution)/shard_map/ppermute | solution.py:265
  19.3 1.4 %collective-permute-start.5 = (bf16[48,1536]{1,0:T(8,128)(2,1)S(1)}, bf16[48,1536]{1,0:T(8,128)(2,1)S(1)}, u32[]{:S(2)}, u32[]{:S(2)}) collective-permute-start(bf16[48,1536]{1,0:T(8,128)(2,1)S(1)} %collective-permute-done.1.refs_2_), channel_id=1, source_target_pairs={{0,4},{4,0},{8,12},{12,8},{16,20},{20,16},{24,28},{28,24},{1,5},{5... | collective-permute-start | bytes 442376 | tf_op jit(solution)/shard_map/ppermute | solution.py:265
  19.3 1.6 %collective-permute-start.6 = (bf16[48,1536]{1,0:T(8,128)(2,1)S(1)}, bf16[48,1536]{1,0:T(8,128)(2,1)S(1)}, u32[]{:S(2)}, u32[]{:S(2)}) collective-permute-start(bf16[48,1536]{1,0:T(8,128)(2,1)S(1)} %collective-permute-done.2.refs_3_), channel_id=1, source_target_pairs={{0,4},{4,0},{8,12},{12,8},{16,20},{20,16},{24,28},{28,24},{1,5},{5... | collective-permute-start | bytes 442376 | tf_op jit(solution)/shard_map/ppermute | solution.py:265
  22.5 9.8 %collective-permute-start.7 = (bf16[96,768]{1,0:T(8,128)(2,1)S(1)}, bf16[96,768]{1,0:T(8,128)(2,1)S(1)}, u32[]{:S(2)}, u32[]{:S(2)}) collective-permute-start(bf16[96,768]{1,0:T(8,128)(2,1)S(1)} %get-tuple-element.98), channel_id=1, source_target_pairs={{0,1},{1,0},{2,3},{3,2},{4,5},{5,4},{6,7},{7,6},{8,9},{9,8},{10,11... | collective-permute-start | bytes 442376 | tf_op jit(solution)/shard_map/ppermute | solution.py:265
  24.2 14.0 %collective-permute-start.8 = (bf16[96,768]{1,0:T(8,128)(2,1)S(1)}, bf16[96,768]{1,0:T(8,128)(2,1)S(1)}, u32[]{:S(2)}, u32[]{:S(2)}) collective-permute-start(bf16[96,768]{1,0:T(8,128)(2,1)S(1)} %get-tuple-element.99), channel_id=1, source_target_pairs={{0,2},{1,3},{2,0},{3,1},{4,6},{5,7},{6,4},{7,5},{8,10},{9,11},{10,... | collective-permute-start | bytes 442376 | tf_op jit(solution)/shard_map/ppermute | solution.py:265
  26.7 11.4 %collective-permute-start.9 = (bf16[96,768]{1,0:T(8,128)(2,1)S(1)}, bf16[96,768]{1,0:T(8,128)(2,1)S(1)}, u32[]{:S(2)}, u32[]{:S(2)}) collective-permute-start(bf16[96,768]{1,0:T(8,128)(2,1)S(1)} %get-tuple-element.100), channel_id=1, source_target_pairs={{0,3},{1,2},{2,1},{3,0},{4,7},{5,6},{6,5},{7,4},{8,11},{9,10},{10,... | collective-permute-start | bytes 442376 | tf_op jit(solution)/shard_map/ppermute | solution.py:265
  27.0 5.3 %copy-start = (bf16[96,768]{1,0:T(8,128)(2,1)S(1)}, bf16[96,768]{1,0:T(8,128)(2,1)}, u32[]{:S(2)}) copy-start(bf16[96,768]{1,0:T(8,128)(2,1)} %param.13) | copy-start | bytes 442372
  38.5 8.2 %collective-permute-start.10 = (bf16[64,768]{1,0:T(8,128)(2,1)S(1)}, bf16[64,768]{1,0:T(8,128)(2,1)S(1)}, u32[]{:S(2)}, u32[]{:S(2)}) collective-permute-start(bf16[64,768]{1,0:T(8,128)(2,1)S(1)} %get-tuple-element.158), channel_id=1, source_target_pairs={{0,1},{1,0},{2,3},{3,2},{4,5},{5,4},{6,7},{7,6},{8,9},{9,8},{10,11... | collective-permute-start | bytes 294920 | tf_op jit(solution)/shard_map/ppermute | solution.py:265
  41.3 9.8 %collective-permute-start.11 = (bf16[64,768]{1,0:T(8,128)(2,1)S(1)}, bf16[64,768]{1,0:T(8,128)(2,1)S(1)}, u32[]{:S(2)}, u32[]{:S(2)}) collective-permute-start(bf16[64,768]{1,0:T(8,128)(2,1)S(1)} %get-tuple-element.157), channel_id=1, source_target_pairs={{0,2},{1,3},{2,0},{3,1},{4,6},{5,7},{6,4},{7,5},{8,10},{9,11},{10,... | collective-permute-start | bytes 294920 | tf_op jit(solution)/shard_map/ppermute | solution.py:265
  42.4 8.7 %collective-permute-start.12 = (bf16[64,768]{1,0:T(8,128)(2,1)S(1)}, bf16[64,768]{1,0:T(8,128)(2,1)S(1)}, u32[]{:S(2)}, u32[]{:S(2)}) collective-permute-start(bf16[64,768]{1,0:T(8,128)(2,1)S(1)} %get-tuple-element.156), channel_id=1, source_target_pairs={{0,3},{1,2},{2,1},{3,0},{4,7},{5,6},{6,5},{7,4},{8,11},{9,10},{10,... | collective-permute-start | bytes 294920 | tf_op jit(solution)/shard_map/ppermute | solution.py:265
  43.8 7.3 %collective-permute-start.13 = (bf16[64,768]{1,0:T(8,128)(2,1)S(1)}, bf16[64,768]{1,0:T(8,128)(2,1)S(1)}, u32[]{:S(2)}, u32[]{:S(2)}) collective-permute-start(bf16[64,768]{1,0:T(8,128)(2,1)S(1)} %get-tuple-element.155), channel_id=1, source_target_pairs={{0,8},{4,12},{8,0},{12,4},{16,24},{20,28},{24,16},{28,20},{1,9},{5... | collective-permute-start | bytes 294920 | tf_op jit(solution)/shard_map/ppermute | solution.py:265
  45.2 6.0 %collective-permute-start.14 = (bf16[64,768]{1,0:T(8,128)(2,1)S(1)}, bf16[64,768]{1,0:T(8,128)(2,1)S(1)}, u32[]{:S(2)}, u32[]{:S(2)}) collective-permute-start(bf16[64,768]{1,0:T(8,128)(2,1)S(1)} %get-tuple-element.155), channel_id=1, source_target_pairs={{0,16},{4,20},{8,24},{12,28},{16,0},{20,4},{24,8},{28,12},{1,17},{... | collective-permute-start | bytes 294920 | tf_op jit(solution)/shard_map/ppermute | solution.py:265
  46.7 5.5 %collective-permute-start.15 = (bf16[64,768]{1,0:T(8,128)(2,1)S(1)}, bf16[64,768]{1,0:T(8,128)(2,1)S(1)}, u32[]{:S(2)}, u32[]{:S(2)}) collective-permute-start(bf16[64,768]{1,0:T(8,128)(2,1)S(1)} %get-tuple-element.155), channel_id=1, source_target_pairs={{0,24},{4,28},{8,16},{12,20},{16,8},{20,12},{24,0},{28,4},{1,25},{... | collective-permute-start | bytes 294920 | tf_op jit(solution)/shard_map/ppermute | solution.py:265
  52.3 9.5 %collective-permute-start.19 = (bf16[256,768]{1,0:T(8,128)(2,1)S(1)}, bf16[256,768]{1,0:T(8,128)(2,1)S(1)}, u32[]{:S(2)}, u32[]{:S(2)}) collective-permute-start(bf16[256,768]{1,0:T(8,128)(2,1)S(1)} %pad_maximum_fusion), channel_id=1, source_target_pairs={{0,4},{4,0},{8,12},{12,8},{16,20},{20,16},{24,28},{28,24},{1,5},{5... | collective-permute-start | bytes 1179656 | tf_op jit(solution)/shard_map/ppermute | solution.py:265
  52.3 11.3 %collective-permute-start.18 = (bf16[192,768]{1,0:T(8,128)(2,1)S(1)}, bf16[192,768]{1,0:T(8,128)(2,1)S(1)}, u32[]{:S(2)}, u32[]{:S(2)}) collective-permute-start(bf16[192,768]{1,0:T(8,128)(2,1)S(1)} %pad_maximum_fusion.2.refs_0_), channel_id=1, source_target_pairs={{0,8},{4,12},{8,0},{12,4},{16,24},{20,28},{24,16},{28,20},{1,9},{5... | collective-permute-start | bytes 884744 | tf_op jit(solution)/shard_map/ppermute | solution.py:265
  53.1 15.4 %collective-permute-start.17 = (bf16[192,768]{1,0:T(8,128)(2,1)S(1)}, bf16[192,768]{1,0:T(8,128)(2,1)S(1)}, u32[]{:S(2)}, u32[]{:S(2)}) collective-permute-start(bf16[192,768]{1,0:T(8,128)(2,1)S(1)} %pad_maximum_fusion.2.refs_0_), channel_id=1, source_target_pairs={{0,16},{4,20},{8,24},{12,28},{16,0},{20,4},{24,8},{28,12},{1,17},{... | collective-permute-start | bytes 884744 | tf_op jit(solution)/shard_map/ppermute | solution.py:265
  54.2 17.2 %collective-permute-start.16 = (bf16[192,768]{1,0:T(8,128)(2,1)S(1)}, bf16[192,768]{1,0:T(8,128)(2,1)S(1)}, u32[]{:S(2)}, u32[]{:S(2)}) collective-permute-start(bf16[192,768]{1,0:T(8,128)(2,1)S(1)} %pad_maximum_fusion.2.refs_0_), channel_id=1, source_target_pairs={{0,24},{4,28},{8,16},{12,20},{16,8},{20,12},{24,0},{28,4},{1,25},{... | collective-permute-start | bytes 884744 | tf_op jit(solution)/shard_map/ppermute | solution.py:265
  63.7 1.8 %collective-permute-start.20 = (bf16[256,768]{1,0:T(8,128)(2,1)S(1)}, bf16[256,768]{1,0:T(8,128)(2,1)S(1)}, u32[]{:S(2)}, u32[]{:S(2)}) collective-permute-start(bf16[256,768]{1,0:T(8,128)(2,1)S(1)} %constant_dynamic-update-slice_fusion), channel_id=1, source_target_pairs={{0,4},{4,0},{8,12},{12,8},{16,20},{20,16},{24,28},{28,24},{1,5},{5... | collective-permute-start | bytes 1179656 | tf_op jit(solution)/shard_map/ppermute | solution.py:265
  68.5 1.8 %collective-permute-start.21 = (bf16[256,768]{1,0:T(8,128)(2,1)S(1)}, bf16[256,768]{1,0:T(8,128)(2,1)S(1)}, u32[]{:S(2)}, u32[]{:S(2)}) collective-permute-start(bf16[256,768]{1,0:T(8,128)(2,1)S(1)} %constant_dynamic-update-slice_fusion.2), channel_id=1, source_target_pairs={{0,4},{4,0},{8,12},{12,8},{16,20},{20,16},{24,28},{28,24},{1,5},{5... | collective-permute-start | bytes 1179656 | tf_op jit(solution)/shard_map/ppermute | solution.py:265
  71.5 1.8 %collective-permute-start.22 = (bf16[256,768]{1,0:T(8,128)(2,1)S(1)}, bf16[256,768]{1,0:T(8,128)(2,1)S(1)}, u32[]{:S(2)}, u32[]{:S(2)}) collective-permute-start(bf16[256,768]{1,0:T(8,128)(2,1)S(1)} %constant_dynamic-update-slice_fusion.4), channel_id=1, source_target_pairs={{0,4},{4,0},{8,12},{12,8},{16,20},{20,16},{24,28},{28,24},{1,5},{5... | collective-permute-start | bytes 1179656 | tf_op jit(solution)/shard_map/ppermute | solution.py:265
  75.4 1.8 %collective-permute-start.23 = (bf16[256,768]{1,0:T(8,128)(2,1)S(1)}, bf16[256,768]{1,0:T(8,128)(2,1)S(1)}, u32[]{:S(2)}, u32[]{:S(2)}) collective-permute-start(bf16[256,768]{1,0:T(8,128)(2,1)S(1)} %fusion.75), channel_id=1, source_target_pairs={{0,4},{4,0},{8,12},{12,8},{16,20},{20,16},{24,28},{28,24},{1,5},{5... | collective-permute-start | bytes 1179656 | tf_op jit(solution)/shard_map/ppermute | solution.py:265
  76.2 1.8 %collective-permute-start.24 = (bf16[256,768]{1,0:T(8,128)(2,1)S(1)}, bf16[256,768]{1,0:T(8,128)(2,1)S(1)}, u32[]{:S(2)}, u32[]{:S(2)}) collective-permute-start(bf16[256,768]{1,0:T(8,128)(2,1)S(1)} %fusion.78), channel_id=1, source_target_pairs={{0,4},{4,0},{8,12},{12,8},{16,20},{20,16},{24,28},{28,24},{1,5},{5... | collective-permute-start | bytes 1179656 | tf_op jit(solution)/shard_map/ppermute | solution.py:265
  79.2 4.1 %collective-permute-start.28 = (bf16[256,768]{1,0:T(8,128)(2,1)S(1)}, bf16[256,768]{1,0:T(8,128)(2,1)S(1)}, u32[]{:S(2)}, u32[]{:S(2)}) collective-permute-start(bf16[256,768]{1,0:T(8,128)(2,1)S(1)} %fusion.84), channel_id=1, source_target_pairs={{0,4},{4,0},{8,12},{12,8},{16,20},{20,16},{24,28},{28,24},{1,5},{5... | collective-permute-start | bytes 1179656 | tf_op jit(solution)/shard_map/ppermute | solution.py:265
  80.2 4.4 %collective-permute-start.25 = (bf16[256,768]{1,0:T(8,128)(2,1)S(1)}, bf16[256,768]{1,0:T(8,128)(2,1)S(1)}, u32[]{:S(2)}, u32[]{:S(2)}) collective-permute-start(bf16[256,768]{1,0:T(8,128)(2,1)S(1)} %fusion.81), channel_id=1, source_target_pairs={{0,4},{4,0},{8,12},{12,8},{16,20},{20,16},{24,28},{28,24},{1,5},{5... | collective-permute-start | bytes 1179656 | tf_op jit(solution)/shard_map/ppermute | solution.py:265
  80.4 15.6 %collective-permute-start.27 = (bf16[192,768]{1,0:T(8,128)(2,1)S(1)}, bf16[192,768]{1,0:T(8,128)(2,1)S(1)}, u32[]{:S(2)}, u32[]{:S(2)}) collective-permute-start(bf16[192,768]{1,0:T(8,128)(2,1)S(1)} %slice.175), channel_id=1, source_target_pairs={{0,16},{4,20},{8,24},{12,28},{16,0},{20,4},{24,8},{28,12},{1,17},{... | collective-permute-start | bytes 884744 | tf_op jit(solution)/shard_map/ppermute | solution.py:265
  80.4 15.6 %collective-permute-start.26 = (bf16[192,768]{1,0:T(8,128)(2,1)S(1)}, bf16[192,768]{1,0:T(8,128)(2,1)S(1)}, u32[]{:S(2)}, u32[]{:S(2)}) collective-permute-start(bf16[192,768]{1,0:T(8,128)(2,1)S(1)} %slice.173), channel_id=1, source_target_pairs={{0,24},{4,28},{8,16},{12,20},{16,8},{20,12},{24,0},{28,4},{1,25},{... | collective-permute-start | bytes 884744 | tf_op jit(solution)/shard_map/ppermute | solution.py:265
  83.9 21.5 %copy-start.1 = (f32[96,2]{0,1:T(2,128)S(1)}, f32[96,2]{0,1:T(2,128)}, u32[]{:S(2)}) copy-start(f32[96,2]{0,1:T(2,128)} %param.22) | copy-start | bytes 2308
  83.9 13.3 %collective-permute-start.29 = (bf16[192,768]{1,0:T(8,128)(2,1)S(1)}, bf16[192,768]{1,0:T(8,128)(2,1)S(1)}, u32[]{:S(2)}, u32[]{:S(2)}) collective-permute-start(bf16[192,768]{1,0:T(8,128)(2,1)S(1)} %slice.178), channel_id=1, source_target_pairs={{0,8},{4,12},{8,0},{12,4},{16,24},{20,28},{24,16},{28,20},{1,9},{5... | collective-permute-start | bytes 884744 | tf_op jit(solution)/shard_map/ppermute | solution.py:265
  97.5 7.3 %collective-permute-start.30 = (bf16[64,768]{1,0:T(8,128)(2,1)S(1)}, bf16[64,768]{1,0:T(8,128)(2,1)S(1)}, u32[]{:S(2)}, u32[]{:S(2)}) collective-permute-start(bf16[64,768]{1,0:T(8,128)(2,1)S(1)} %get-tuple-element.161), channel_id=1, source_target_pairs={{0,1},{1,0},{2,3},{3,2},{4,5},{5,4},{6,7},{7,6},{8,9},{9,8},{10,11... | collective-permute-start | bytes 294920 | tf_op jit(solution)/shard_map/ppermute | solution.py:265
  98.8 9.8 %collective-permute-start.31 = (bf16[64,768]{1,0:T(8,128)(2,1)S(1)}, bf16[64,768]{1,0:T(8,128)(2,1)S(1)}, u32[]{:S(2)}, u32[]{:S(2)}) collective-permute-start(bf16[64,768]{1,0:T(8,128)(2,1)S(1)} %get-tuple-element.160), channel_id=1, source_target_pairs={{0,2},{1,3},{2,0},{3,1},{4,6},{5,7},{6,4},{7,5},{8,10},{9,11},{10,... | collective-permute-start | bytes 294920 | tf_op jit(solution)/shard_map/ppermute | solution.py:265
  100.5 8.1 %collective-permute-start.32 = (bf16[64,768]{1,0:T(8,128)(2,1)S(1)}, bf16[64,768]{1,0:T(8,128)(2,1)S(1)}, u32[]{:S(2)}, u32[]{:S(2)}) collective-permute-start(bf16[64,768]{1,0:T(8,128)(2,1)S(1)} %get-tuple-element.159), channel_id=1, source_target_pairs={{0,3},{1,2},{2,1},{3,0},{4,7},{5,6},{6,5},{7,4},{8,11},{9,10},{10,... | collective-permute-start | bytes 294920 | tf_op jit(solution)/shard_map/ppermute | solution.py:265
  101.9 6.7 %collective-permute-start.33 = (bf16[64,768]{1,0:T(8,128)(2,1)S(1)}, bf16[64,768]{1,0:T(8,128)(2,1)S(1)}, u32[]{:S(2)}, u32[]{:S(2)}) collective-permute-start(bf16[64,768]{1,0:T(8,128)(2,1)S(1)} %slice.172), channel_id=1, source_target_pairs={{0,24},{4,28},{8,16},{12,20},{16,8},{20,12},{24,0},{28,4},{1,25},{... | collective-permute-start | bytes 294920 | tf_op jit(solution)/shard_map/ppermute | solution.py:265
  103.2 5.4 %collective-permute-start.34 = (bf16[64,768]{1,0:T(8,128)(2,1)S(1)}, bf16[64,768]{1,0:T(8,128)(2,1)S(1)}, u32[]{:S(2)}, u32[]{:S(2)}) collective-permute-start(bf16[64,768]{1,0:T(8,128)(2,1)S(1)} %slice.174), channel_id=1, source_target_pairs={{0,16},{4,20},{8,24},{12,28},{16,0},{20,4},{24,8},{28,12},{1,17},{... | collective-permute-start | bytes 294920 | tf_op jit(solution)/shard_map/ppermute | solution.py:265
  104.7 4.6 %collective-permute-start.35 = (bf16[64,768]{1,0:T(8,128)(2,1)S(1)}, bf16[64,768]{1,0:T(8,128)(2,1)S(1)}, u32[]{:S(2)}, u32[]{:S(2)}) collective-permute-start(bf16[64,768]{1,0:T(8,128)(2,1)S(1)} %slice.179), channel_id=1, source_target_pairs={{0,8},{4,12},{8,0},{12,4},{16,24},{20,28},{24,16},{28,20},{1,9},{5... | collective-permute-start | bytes 294920 | tf_op jit(solution)/shard_map/ppermute | solution.py:265

commit v3 on v2

--- a/solution.py
+++ b/solution.py
@@ -346,11 +346,17 @@
         pick, hidden_in, (((0,), (0,)), ((), ())), preferred_element_type=f32
     ).astype(bf16)
     buffers = buffers.reshape(experts, slots, width)
-    first = {k: swap(buffers[0], "section", 2 * k) for k in range(1, chips)}
-    rest = jnp.concatenate(exchange(buffers), axis=0)
-    rest, first = lax.optimization_barrier((rest, first))
-    down_parts = fetch(w_down, 1, found, rest)
-    received = jnp.concatenate([buffers[0], rest], axis=0)
+    half = experts // 2
+    arrived = {0: buffers[0]}
+    for k in [*range(1, half), *reversed(range(half, experts))]:
+        arrived[k] = swap(buffers[k], "expert", k)
+    near = jnp.concatenate([arrived[k] for k in range(half)], axis=0)
+    first = {k: swap(near, "section", 2 * k) for k in range(1, chips)}
+    rest = jnp.concatenate([arrived[k] for k in range(half, experts)], axis=0)
+    rest, first, down_parts = lax.optimization_barrier(
+        (rest, first, fetch(w_down, 1, found, near))
+    )
+    received = jnp.concatenate([near, rest], axis=0)
     second = {k: swap(rest, "section", 2 * k) for k in range(1, chips)}
 
     sums = []

time: 111 us -> 109 us (0.982)
  waiting for transfers between devices: 32.4 us -> 29.9 us
    ppermute x36, waiting for transfers between devices: 32.4 us -> 29.9 us  [swap(): return lax.ppermute(value, axis, [(i, i ^ mask) for i in range(size)])]
where the time goes in v3:
time: 109 us
  starting transfers between devices  36.5 us (33%)
  waiting for transfers between devices  29.9 us (27%)
  Pallas kernels  24.7 us (23%)
  matrix products  16.1 us (15%)
  other arithmetic  1.25 us (1%)
    ppermute x36, starting transfers between devices, swap(): return lax.ppermute(value, axis, [(i, i ^ mask) for i in range(size)])  36.5 us
    ppermute x36, waiting for transfers between devices, swap(): return lax.ppermute(value, axis, [(i, i ^ mask) for i in range(size)])  29.9 us
    dot_general x27, matrix products, dot(): return jnp.dot(a, b, preferred_element_type=jnp.float32)  15.8 us
    pallas_call x3, Pallas kernels, fetch(): pl.pallas_call(functools.partial(fetch_kernel, dim, count), in_specs=[pl....  15.8 us
    pallas_call x1, Pallas kernels, attend(): pl.pallas_call(functools.partial(attend_kernel, rows // requests), in_spe...  7.26 us
  transfers between devices with their start and end apart: 36, of which 18 were waited for; matrix products, arithmetic and copies ran while one was open for 11% of the time, Pallas kernels for 14%

profile of v3, /device:TPU:0, one launch (start us, length us, event | category | flops | bytes accessed | tf_op | source)
XLA Modules:
  0.0 109.3 jit_solution(13887539368810022394)
XLA Ops:
  0.0 7.3 %attend.1 = (bf16[48,1536]{1,0:T(8,128)(2,1)S(1)}, bf16[1536,768]{1,0:T(8,128)(2,1)S(1)}) custom-call(s32[8]{0:T(128)} %len_hbm.1, bf16[48,1536]{1,0:T(8,128)(2,1)} %q_hbm.1, bf16[48,256]{1,0:T(8,128)(2,1)} %nk_hbm.1, bf16[48,256]{1,0:T(8,128)(2,1)} %nv_hbm.1, bf16[8,1024,256]{2,1,0:T(8,128)(2,1)} %ck_hbm.1, bf16[8,1024,256]{2,1,0:T(8,128)(2,1)} %cv_hbm.1, ...), custom_call_target="tpu_custom_call" | custom-call | flops 301989888 | bytes 8388608 | tf_op jit(solution)/shard_map/attend/pallas_call | solution.py:150
  7.3 3.0 %collective-permute-start = (bf16[48,1536]{1,0:T(8,128)(2,1)S(1)}, bf16[48,1536]{1,0:T(8,128)(2,1)S(1)}, u32[]{:S(2)}, u32[]{:S(2)}) collective-permute-start(bf16[48,1536]{1,0:T(8,128)(2,1)S(1)} %get-tuple-element.91.refs_0_), channel_id=1, source_target_pairs={{0,8},{4,12},{8,0},{12,4},{16,24},{20,28},{24,16},{28,20},{1,9},{5... | collective-permute-start | bytes 442376 | tf_op jit(solution)/shard_map/ppermute | solution.py:265
  10.3 1.5 %collective-permute-start.1 = (bf16[48,1536]{1,0:T(8,128)(2,1)S(1)}, bf16[48,1536]{1,0:T(8,128)(2,1)S(1)}, u32[]{:S(2)}, u32[]{:S(2)}) collective-permute-start(bf16[48,1536]{1,0:T(8,128)(2,1)S(1)} %get-tuple-element.91.refs_0_), channel_id=1, source_target_pairs={{0,16},{4,20},{8,24},{12,28},{16,0},{20,4},{24,8},{28,12},{1,17},{... | collective-permute-start | bytes 442376 | tf_op jit(solution)/shard_map/ppermute | solution.py:265
  11.8 0.8 dynamic-slice_xor_fusion
  12.7 5.2 %fetch.3 = (bf16[1536,1024]{1,0:T(8,128)(2,1)S(1)}, bf16[1536,1024]{1,0:T(8,128)(2,1)S(1)}, bf16[1536,1024]{1,0:T(8,128)(2,1)S(1)}, bf16[1536,1024]{1,0:T(8,128)(2,1)S(1)}) custom-call(s32[8]{0:T(128)S(1)} %get-tuple-element.86.at_ref, bf16[1,6144,1024]{2,1,0:T(8,128)(2,1)} %src.3, bf16[48,1536]{1,0:T(8,128)(2,1)S(1)} %get-tuple-element.91.refs_0_), custom_call_target="tpu_custom_call" | custom-call | bytes 12582912 | tf_op jit(solution)/shard_map/fetch/pallas_call | solution.py:248
  18.1 0.7 collective-permute-done.1.refs_2_
  18.7 0.5 collective-permute-start.4
  19.3 0.5 collective-permute-start.6
  20.8 1.7 %project.1 = (f32[96,768]{1,0:T(8,128)S(1)}, bf16[96,768]{1,0:T(8,128)(2,1)S(1)}, bf16[96,768]{1,0:T(8,128)(2,1)S(1)}, bf16[96,768]{1,0:T(8,128)(2,1)S(1)}) custom-call(s32[8]{0:T(128)S(1)} %get-tuple-element.84.at_ref, bf16[48,1536]{1,0:T(8,128)(2,1)S(1)} %get-tuple-element.91.refs_0_, bf16[48,1536]{1,0:T(8,128)(2,1)S(1)} %collective-permute-done.refs_1_, ...), custom_call_target="tpu_custom_call" | custom-call | flops 905969664 | bytes 2359296 | tf_op jit(solution)/shard_map/project/pallas_call | solution.py:207
  22.5 1.6 %collective-permute-start.7 = (bf16[96,768]{1,0:T(8,128)(2,1)S(1)}, bf16[96,768]{1,0:T(8,128)(2,1)S(1)}, u32[]{:S(2)}, u32[]{:S(2)}) collective-permute-start(bf16[96,768]{1,0:T(8,128)(2,1)S(1)} %get-tuple-element.102), channel_id=1, source_target_pairs={{0,1},{1,0},{2,3},{3,2},{4,5},{5,4},{6,7},{7,6},{8,9},{9,8},{10,11... | collective-permute-start | bytes 442376 | tf_op jit(solution)/shard_map/ppermute | solution.py:265
  24.2 2.6 %collective-permute-start.8 = (bf16[96,768]{1,0:T(8,128)(2,1)S(1)}, bf16[96,768]{1,0:T(8,128)(2,1)S(1)}, u32[]{:S(2)}, u32[]{:S(2)}) collective-permute-start(bf16[96,768]{1,0:T(8,128)(2,1)S(1)} %get-tuple-element.103), channel_id=1, source_target_pairs={{0,2},{1,3},{2,0},{3,1},{4,6},{5,7},{6,4},{7,5},{8,10},{9,11},{10,... | collective-permute-start | bytes 442376 | tf_op jit(solution)/shard_map/ppermute | solution.py:265
  27.0 5.2 %fetch.4 = (bf16[1536,1024]{1,0:T(8,128)(2,1)S(1)}, bf16[1536,1024]{1,0:T(8,128)(2,1)S(1)}, bf16[1536,1024]{1,0:T(8,128)(2,1)S(1)}, bf16[1536,1024]{1,0:T(8,128)(2,1)S(1)}) custom-call(s32[8]{0:T(128)S(1)} %get-tuple-element.86.at_ref, bf16[1,6144,1024]{2,1,0:T(8,128)(2,1)} %src.4, f32[96,768]{1,0:T(8,128)S(1)} %get-tuple-element.96.refs_0_), custom_call_target="tpu_custom_call" | custom-call | bytes 12582912 | tf_op jit(solution)/shard_map/fetch/pallas_call | solution.py:248
  32.3 5.9 %collective-permute-done.8 = bf16[96,768]{1,0:T(8,128)(2,1)S(1)} collective-permute-done((bf16[96,768]{1,0:T(8,128)(2,1)S(1)}, bf16[96,768]{1,0:T(8,128)(2,1)S(1)}, u32[]{:S(2)}, u32[]{:S(2)}) %collective-permute-start.8) | collective-permute-done | bytes 147488 | tf_op jit(solution)/shard_map/ppermute | solution.py:265
  38.5 2.8 %collective-permute-start.12 = (bf16[64,768]{1,0:T(8,128)(2,1)S(1)}, bf16[64,768]{1,0:T(8,128)(2,1)S(1)}, u32[]{:S(2)}, u32[]{:S(2)}) collective-permute-start(bf16[64,768]{1,0:T(8,128)(2,1)S(1)} %get-tuple-element.164), channel_id=1, source_target_pairs={{0,1},{1,0},{2,3},{3,2},{4,5},{5,4},{6,7},{7,6},{8,9},{9,8},{10,11... | collective-permute-start | bytes 294920 | tf_op jit(solution)/shard_map/ppermute | solution.py:265
  41.3 1.1 collective-permute-start.10
  42.4 1.4 %collective-permute-start.11 = (bf16[64,768]{1,0:T(8,128)(2,1)S(1)}, bf16[64,768]{1,0:T(8,128)(2,1)S(1)}, u32[]{:S(2)}, u32[]{:S(2)}) collective-permute-start(bf16[64,768]{1,0:T(8,128)(2,1)S(1)} %get-tuple-element.165), channel_id=1, source_target_pairs={{0,3},{1,2},{2,1},{3,0},{4,7},{5,6},{6,5},{7,4},{8,11},{9,10},{10,... | collective-permute-start | bytes 294920 | tf_op jit(solution)/shard_map/ppermute | solution.py:265
  43.8 1.1 %collective-permute-done.12 = bf16[64,768]{1,0:T(8,128)(2,1)S(1)} collective-permute-done((bf16[64,768]{1,0:T(8,128)(2,1)S(1)}, bf16[64,768]{1,0:T(8,128)(2,1)S(1)}, u32[]{:S(2)}, u32[]{:S(2)}) %collective-permute-start.12) | collective-permute-done | bytes 98336 | tf_op jit(solution)/shard_map/ppermute | solution.py:265
  44.9 1.4 %collective-permute-start.13 = (bf16[128,768]{1,0:T(8,128)(2,1)S(1)}, bf16[128,768]{1,0:T(8,128)(2,1)S(1)}, u32[]{:S(2)}, u32[]{:S(2)}) collective-permute-start(bf16[128,768]{1,0:T(8,128)(2,1)S(1)} %pad_maximum_fusion.3.refs_0_), channel_id=1, source_target_pairs={{0,8},{4,12},{8,0},{12,4},{16,24},{20,28},{24,16},{28,20},{1,9},{5... | collective-permute-start | bytes 589832 | tf_op jit(solution)/shard_map/ppermute | solution.py:265
  46.4 1.5 %collective-permute-start.14 = (bf16[128,768]{1,0:T(8,128)(2,1)S(1)}, bf16[128,768]{1,0:T(8,128)(2,1)S(1)}, u32[]{:S(2)}, u32[]{:S(2)}) collective-permute-start(bf16[128,768]{1,0:T(8,128)(2,1)S(1)} %pad_maximum_fusion.3.refs_0_), channel_id=1, source_target_pairs={{0,16},{4,20},{8,24},{12,28},{16,0},{20,4},{24,8},{28,12},{1,17},{... | collective-permute-start | bytes 589832 | tf_op jit(solution)/shard_map/ppermute | solution.py:265
  47.9 0.6 collective-permute-start.15
  48.5 5.3 %fetch.5 = (bf16[1024,1536]{1,0:T(8,128)(2,1)S(1)}, bf16[1024,1536]{1,0:T(8,128)(2,1)S(1)}, bf16[1024,1536]{1,0:T(8,128)(2,1)S(1)}, bf16[1024,1536]{1,0:T(8,128)(2,1)S(1)}) custom-call(s32[8]{0:T(128)S(1)} %get-tuple-element.86.at_ref, bf16[1,1024,6144]{2,1,0:T(8,128)(2,1)} %src.5, bf16[128,768]{1,0:T(8,128)(2,1)S(1)} %pad_maximum_fusion.3.refs_0_), custom_call_target="tpu_custom_call" | custom-call | bytes 12582912 | tf_op jit(solution)/shard_map/fetch/pallas_call | solution.py:248
  53.8 1.0 collective-permute-done.14
  55.0 1.1 collective-permute-start.18
  56.0 0.9 collective-permute-start.17
  57.0 1.5 %collective-permute-start.16 = (bf16[128,768]{1,0:T(8,128)(2,1)S(1)}, bf16[128,768]{1,0:T(8,128)(2,1)S(1)}, u32[]{:S(2)}, u32[]{:S(2)}) collective-permute-start(bf16[128,768]{1,0:T(8,128)(2,1)S(1)} %pad_maximum_fusion.2), channel_id=1, source_target_pairs={{0,24},{4,28},{8,16},{12,20},{16,8},{20,12},{24,0},{28,4},{1,25},{... | collective-permute-start | bytes 589832 | tf_op jit(solution)/shard_map/ppermute | solution.py:265
  58.5 0.6 fusion.40
  59.1 0.6 fusion.51
  59.7 0.6 fusion.44
  60.3 0.6 fusion.48
  60.9 1.8 %collective-permute-done.18 = bf16[128,768]{1,0:T(8,128)(2,1)S(1)} collective-permute-done((bf16[128,768]{1,0:T(8,128)(2,1)S(1)}, bf16[128,768]{1,0:T(8,128)(2,1)S(1)}, u32[]{:S(2)}, u32[]{:S(2)}) %collective-permute-start.18) | collective-permute-done | bytes 196640 | tf_op jit(solution)/shard_map/ppermute | solution.py:265
  62.9 0.6 fusion.34
  63.4 0.6 fusion.38
  64.0 0.6 collective-permute-done.20
  64.6 0.6 add_add_fusion.2
  65.2 0.6 add_add_fusion.3
  66.0 0.6 fusion.26
  66.6 0.6 fusion.30
  67.6 0.6 add_add_fusion
  68.2 0.6 add_add_fusion.1
  69.0 0.6 fusion.22
  69.6 0.6 fusion.18
  70.6 0.6 fusion.20
  71.2 1.0 multiply_convert_fusion
  72.3 0.6 fusion.75
  73.1 0.6 fusion.78
  73.7 0.5 collective-permute-start.24
  74.2 0.5 collective-permute-done.23
  74.7 0.6 fusion.72
  75.5 0.6 fusion.69
  76.1 0.6 fusion.84
  77.2 0.6 fusion.81
  78.0 2.4 %collective-permute-start.27 = (bf16[192,768]{1,0:T(8,128)(2,1)S(1)}, bf16[192,768]{1,0:T(8,128)(2,1)S(1)}, u32[]{:S(2)}, u32[]{:S(2)}) collective-permute-start(bf16[192,768]{1,0:T(8,128)(2,1)S(1)} %slice.172), channel_id=1, source_target_pairs={{0,16},{4,20},{8,24},{12,28},{16,0},{20,4},{24,8},{28,12},{1,17},{... | collective-permute-start | bytes 884744 | tf_op jit(solution)/shard_map/ppermute | solution.py:265
  80.4 1.5 %collective-permute-start.26 = (bf16[192,768]{1,0:T(8,128)(2,1)S(1)}, bf16[192,768]{1,0:T(8,128)(2,1)S(1)}, u32[]{:S(2)}, u32[]{:S(2)}) collective-permute-start(bf16[192,768]{1,0:T(8,128)(2,1)S(1)} %slice.170), channel_id=1, source_target_pairs={{0,24},{4,28},{8,16},{12,20},{16,8},{20,12},{24,0},{28,4},{1,25},{... | collective-permute-start | bytes 884744 | tf_op jit(solution)/shard_map/ppermute | solution.py:265
  82.0 0.6 fusion.66
  82.7 0.6 fusion.60
  83.3 11.0 %collective-permute-done.27 = bf16[192,768]{1,0:T(8,128)(2,1)S(1)} collective-permute-done((bf16[192,768]{1,0:T(8,128)(2,1)S(1)}, bf16[192,768]{1,0:T(8,128)(2,1)S(1)}, u32[]{:S(2)}, u32[]{:S(2)}) %collective-permute-start.27) | collective-permute-done | bytes 294944 | tf_op jit(solution)/shard_map/ppermute | solution.py:265
  94.3 1.2 %collective-permute-done.29 = bf16[192,768]{1,0:T(8,128)(2,1)S(1)} collective-permute-done((bf16[192,768]{1,0:T(8,128)(2,1)S(1)}, bf16[192,768]{1,0:T(8,128)(2,1)S(1)}, u32[]{:S(2)}, u32[]{:S(2)}) %collective-permute-start.29) | collective-permute-done | bytes 294944 | tf_op jit(solution)/shard_map/ppermute | solution.py:265
  95.7 2.1 %collective-permute-start.30 = (bf16[64,768]{1,0:T(8,128)(2,1)S(1)}, bf16[64,768]{1,0:T(8,128)(2,1)S(1)}, u32[]{:S(2)}, u32[]{:S(2)}) collective-permute-start(bf16[64,768]{1,0:T(8,128)(2,1)S(1)} %get-tuple-element.169), channel_id=1, source_target_pairs={{0,1},{1,0},{2,3},{3,2},{4,5},{5,4},{6,7},{7,6},{8,9},{9,8},{10,11... | collective-permute-start | bytes 294920 | tf_op jit(solution)/shard_map/ppermute | solution.py:265
  97.8 1.2 %collective-permute-start.31 = (bf16[64,768]{1,0:T(8,128)(2,1)S(1)}, bf16[64,768]{1,0:T(8,128)(2,1)S(1)}, u32[]{:S(2)}, u32[]{:S(2)}) collective-permute-start(bf16[64,768]{1,0:T(8,128)(2,1)S(1)} %get-tuple-element.168), channel_id=1, source_target_pairs={{0,2},{1,3},{2,0},{3,1},{4,6},{5,7},{6,4},{7,5},{8,10},{9,11},{10,... | collective-permute-start | bytes 294920 | tf_op jit(solution)/shard_map/ppermute | solution.py:265
  99.0 1.4 %collective-permute-start.32 = (bf16[64,768]{1,0:T(8,128)(2,1)S(1)}, bf16[64,768]{1,0:T(8,128)(2,1)S(1)}, u32[]{:S(2)}, u32[]{:S(2)}) collective-permute-start(bf16[64,768]{1,0:T(8,128)(2,1)S(1)} %get-tuple-element.167), channel_id=1, source_target_pairs={{0,3},{1,2},{2,1},{3,0},{4,7},{5,6},{6,5},{7,4},{8,11},{9,10},{10,... | collective-permute-start | bytes 294920 | tf_op jit(solution)/shard_map/ppermute | solution.py:265
  100.4 2.3 %collective-permute-start.33 = (bf16[64,768]{1,0:T(8,128)(2,1)S(1)}, bf16[64,768]{1,0:T(8,128)(2,1)S(1)}, u32[]{:S(2)}, u32[]{:S(2)}) collective-permute-start(bf16[64,768]{1,0:T(8,128)(2,1)S(1)} %slice.169), channel_id=1, source_target_pairs={{0,24},{4,28},{8,16},{12,20},{16,8},{20,12},{24,0},{28,4},{1,25},{... | collective-permute-start | bytes 294920 | tf_op jit(solution)/shard_map/ppermute | solution.py:265
  102.7 0.7 collective-permute-start.34
  103.9 4.0 %collective-permute-done.31 = bf16[64,768]{1,0:T(8,128)(2,1)S(1)} collective-permute-done((bf16[64,768]{1,0:T(8,128)(2,1)S(1)}, bf16[64,768]{1,0:T(8,128)(2,1)S(1)}, u32[]{:S(2)}, u32[]{:S(2)}) %collective-permute-start.31) | collective-permute-done | bytes 98336 | tf_op jit(solution)/shard_map/ppermute | solution.py:265
  108.4 0.9 add_convert_fusion
  (75 shorter events, 5.7 us)
Async XLA Ops:
  7.3 10.8 %collective-permute-start = (bf16[48,1536]{1,0:T(8,128)(2,1)S(1)}, bf16[48,1536]{1,0:T(8,128)(2,1)S(1)}, u32[]{:S(2)}, u32[]{:S(2)}) collective-permute-start(bf16[48,1536]{1,0:T(8,128)(2,1)S(1)} %get-tuple-element.91.refs_0_), channel_id=1, source_target_pairs={{0,8},{4,12},{8,0},{12,4},{16,24},{20,28},{24,16},{28,20},{1,9},{5... | collective-permute-start | bytes 442376 | tf_op jit(solution)/shard_map/ppermute | solution.py:265
  10.3 8.5 %collective-permute-start.1 = (bf16[48,1536]{1,0:T(8,128)(2,1)S(1)}, bf16[48,1536]{1,0:T(8,128)(2,1)S(1)}, u32[]{:S(2)}, u32[]{:S(2)}) collective-permute-start(bf16[48,1536]{1,0:T(8,128)(2,1)S(1)} %get-tuple-element.91.refs_0_), channel_id=1, source_target_pairs={{0,16},{4,20},{8,24},{12,28},{16,0},{20,4},{24,8},{28,12},{1,17},{... | collective-permute-start | bytes 442376 | tf_op jit(solution)/shard_map/ppermute | solution.py:265
  11.8 6.9 %collective-permute-start.2 = (bf16[48,1536]{1,0:T(8,128)(2,1)S(1)}, bf16[48,1536]{1,0:T(8,128)(2,1)S(1)}, u32[]{:S(2)}, u32[]{:S(2)}) collective-permute-start(bf16[48,1536]{1,0:T(8,128)(2,1)S(1)} %get-tuple-element.91.refs_0_), channel_id=1, source_target_pairs={{0,24},{4,28},{8,16},{12,20},{16,8},{20,12},{24,0},{28,4},{1,25},{... | collective-permute-start | bytes 442376 | tf_op jit(solution)/shard_map/ppermute | solution.py:265
  18.7 1.4 %collective-permute-start.3 = (bf16[48,1536]{1,0:T(8,128)(2,1)S(1)}, bf16[48,1536]{1,0:T(8,128)(2,1)S(1)}, u32[]{:S(2)}, u32[]{:S(2)}) collective-permute-start(bf16[48,1536]{1,0:T(8,128)(2,1)S(1)} %get-tuple-element.91.refs_0_), channel_id=1, source_target_pairs={{0,4},{4,0},{8,12},{12,8},{16,20},{20,16},{24,28},{28,24},{1,5},{5... | collective-permute-start | bytes 442376 | tf_op jit(solution)/shard_map/ppermute | solution.py:265
  18.7 1.6 %collective-permute-start.4 = (bf16[48,1536]{1,0:T(8,128)(2,1)S(1)}, bf16[48,1536]{1,0:T(8,128)(2,1)S(1)}, u32[]{:S(2)}, u32[]{:S(2)}) collective-permute-start(bf16[48,1536]{1,0:T(8,128)(2,1)S(1)} %collective-permute-done.refs_1_), channel_id=1, source_target_pairs={{0,4},{4,0},{8,12},{12,8},{16,20},{20,16},{24,28},{28,24},{1,5},{5... | collective-permute-start | bytes 442376 | tf_op jit(solution)/shard_map/ppermute | solution.py:265
  19.3 1.4 %collective-permute-start.5 = (bf16[48,1536]{1,0:T(8,128)(2,1)S(1)}, bf16[48,1536]{1,0:T(8,128)(2,1)S(1)}, u32[]{:S(2)}, u32[]{:S(2)}) collective-permute-start(bf16[48,1536]{1,0:T(8,128)(2,1)S(1)} %collective-permute-done.1.refs_2_), channel_id=1, source_target_pairs={{0,4},{4,0},{8,12},{12,8},{16,20},{20,16},{24,28},{28,24},{1,5},{5... | collective-permute-start | bytes 442376 | tf_op jit(solution)/shard_map/ppermute | solution.py:265
  19.3 1.6 %collective-permute-start.6 = (bf16[48,1536]{1,0:T(8,128)(2,1)S(1)}, bf16[48,1536]{1,0:T(8,128)(2,1)S(1)}, u32[]{:S(2)}, u32[]{:S(2)}) collective-permute-start(bf16[48,1536]{1,0:T(8,128)(2,1)S(1)} %collective-permute-done.2.refs_3_), channel_id=1, source_target_pairs={{0,4},{4,0},{8,12},{12,8},{16,20},{20,16},{24,28},{28,24},{1,5},{5... | collective-permute-start | bytes 442376 | tf_op jit(solution)/shard_map/ppermute | solution.py:265
  22.5 9.8 %collective-permute-start.7 = (bf16[96,768]{1,0:T(8,128)(2,1)S(1)}, bf16[96,768]{1,0:T(8,128)(2,1)S(1)}, u32[]{:S(2)}, u32[]{:S(2)}) collective-permute-start(bf16[96,768]{1,0:T(8,128)(2,1)S(1)} %get-tuple-element.102), channel_id=1, source_target_pairs={{0,1},{1,0},{2,3},{3,2},{4,5},{5,4},{6,7},{7,6},{8,9},{9,8},{10,11... | collective-permute-start | bytes 442376 | tf_op jit(solution)/shard_map/ppermute | solution.py:265
  24.2 14.0 %collective-permute-start.8 = (bf16[96,768]{1,0:T(8,128)(2,1)S(1)}, bf16[96,768]{1,0:T(8,128)(2,1)S(1)}, u32[]{:S(2)}, u32[]{:S(2)}) collective-permute-start(bf16[96,768]{1,0:T(8,128)(2,1)S(1)} %get-tuple-element.103), channel_id=1, source_target_pairs={{0,2},{1,3},{2,0},{3,1},{4,6},{5,7},{6,4},{7,5},{8,10},{9,11},{10,... | collective-permute-start | bytes 442376 | tf_op jit(solution)/shard_map/ppermute | solution.py:265
  26.7 11.4 %collective-permute-start.9 = (bf16[96,768]{1,0:T(8,128)(2,1)S(1)}, bf16[96,768]{1,0:T(8,128)(2,1)S(1)}, u32[]{:S(2)}, u32[]{:S(2)}) collective-permute-start(bf16[96,768]{1,0:T(8,128)(2,1)S(1)} %get-tuple-element.104), channel_id=1, source_target_pairs={{0,3},{1,2},{2,1},{3,0},{4,7},{5,6},{6,5},{7,4},{8,11},{9,10},{10,... | collective-permute-start | bytes 442376 | tf_op jit(solution)/shard_map/ppermute | solution.py:265
  27.0 5.3 %copy-start = (bf16[96,768]{1,0:T(8,128)(2,1)S(1)}, bf16[96,768]{1,0:T(8,128)(2,1)}, u32[]{:S(2)}) copy-start(bf16[96,768]{1,0:T(8,128)(2,1)} %param.13) | copy-start | bytes 442372
  38.5 6.4 %collective-permute-start.12 = (bf16[64,768]{1,0:T(8,128)(2,1)S(1)}, bf16[64,768]{1,0:T(8,128)(2,1)S(1)}, u32[]{:S(2)}, u32[]{:S(2)}) collective-permute-start(bf16[64,768]{1,0:T(8,128)(2,1)S(1)} %get-tuple-element.164), channel_id=1, source_target_pairs={{0,1},{1,0},{2,3},{3,2},{4,5},{5,4},{6,7},{7,6},{8,9},{9,8},{10,11... | collective-permute-start | bytes 294920 | tf_op jit(solution)/shard_map/ppermute | solution.py:265
  41.3 12.5 %collective-permute-start.10 = (bf16[64,768]{1,0:T(8,128)(2,1)S(1)}, bf16[64,768]{1,0:T(8,128)(2,1)S(1)}, u32[]{:S(2)}, u32[]{:S(2)}) collective-permute-start(bf16[64,768]{1,0:T(8,128)(2,1)S(1)} %get-tuple-element.166), channel_id=1, source_target_pairs={{0,2},{1,3},{2,0},{3,1},{4,6},{5,7},{6,4},{7,5},{8,10},{9,11},{10,... | collective-permute-start | bytes 294920 | tf_op jit(solution)/shard_map/ppermute | solution.py:265
  42.4 11.4 %collective-permute-start.11 = (bf16[64,768]{1,0:T(8,128)(2,1)S(1)}, bf16[64,768]{1,0:T(8,128)(2,1)S(1)}, u32[]{:S(2)}, u32[]{:S(2)}) collective-permute-start(bf16[64,768]{1,0:T(8,128)(2,1)S(1)} %get-tuple-element.165), channel_id=1, source_target_pairs={{0,3},{1,2},{2,1},{3,0},{4,7},{5,6},{6,5},{7,4},{8,11},{9,10},{10,... | collective-permute-start | bytes 294920 | tf_op jit(solution)/shard_map/ppermute | solution.py:265
  44.9 8.9 %collective-permute-start.13 = (bf16[128,768]{1,0:T(8,128)(2,1)S(1)}, bf16[128,768]{1,0:T(8,128)(2,1)S(1)}, u32[]{:S(2)}, u32[]{:S(2)}) collective-permute-start(bf16[128,768]{1,0:T(8,128)(2,1)S(1)} %pad_maximum_fusion.3.refs_0_), channel_id=1, source_target_pairs={{0,8},{4,12},{8,0},{12,4},{16,24},{20,28},{24,16},{28,20},{1,9},{5... | collective-permute-start | bytes 589832 | tf_op jit(solution)/shard_map/ppermute | solution.py:265
  46.4 8.5 %collective-permute-start.14 = (bf16[128,768]{1,0:T(8,128)(2,1)S(1)}, bf16[128,768]{1,0:T(8,128)(2,1)S(1)}, u32[]{:S(2)}, u32[]{:S(2)}) collective-permute-start(bf16[128,768]{1,0:T(8,128)(2,1)S(1)} %pad_maximum_fusion.3.refs_0_), channel_id=1, source_target_pairs={{0,16},{4,20},{8,24},{12,28},{16,0},{20,4},{24,8},{28,12},{1,17},{... | collective-permute-start | bytes 589832 | tf_op jit(solution)/shard_map/ppermute | solution.py:265
  47.9 7.0 %collective-permute-start.15 = (bf16[128,768]{1,0:T(8,128)(2,1)S(1)}, bf16[128,768]{1,0:T(8,128)(2,1)S(1)}, u32[]{:S(2)}, u32[]{:S(2)}) collective-permute-start(bf16[128,768]{1,0:T(8,128)(2,1)S(1)} %pad_maximum_fusion.3.refs_0_), channel_id=1, source_target_pairs={{0,24},{4,28},{8,16},{12,20},{16,8},{20,12},{24,0},{28,4},{1,25},{... | collective-permute-start | bytes 589832 | tf_op jit(solution)/shard_map/ppermute | solution.py:265
  54.9 3.6 %collective-permute-start.19 = (bf16[256,768]{1,0:T(8,128)(2,1)S(1)}, bf16[256,768]{1,0:T(8,128)(2,1)S(1)}, u32[]{:S(2)}, u32[]{:S(2)}) collective-permute-start(bf16[256,768]{1,0:T(8,128)(2,1)S(1)} %pad_maximum_fusion), channel_id=1, source_target_pairs={{0,4},{4,0},{8,12},{12,8},{16,20},{20,16},{24,28},{28,24},{1,5},{5... | collective-permute-start | bytes 1179656 | tf_op jit(solution)/shard_map/ppermute | solution.py:265
  55.0 7.8 %collective-permute-start.18 = (bf16[128,768]{1,0:T(8,128)(2,1)S(1)}, bf16[128,768]{1,0:T(8,128)(2,1)S(1)}, u32[]{:S(2)}, u32[]{:S(2)}) collective-permute-start(bf16[128,768]{1,0:T(8,128)(2,1)S(1)} %pad_maximum_fusion.2), channel_id=1, source_target_pairs={{0,8},{4,12},{8,0},{12,4},{16,24},{20,28},{24,16},{28,20},{1,9},{5... | collective-permute-start | bytes 589832 | tf_op jit(solution)/shard_map/ppermute | solution.py:265
  56.0 9.7 %collective-permute-start.17 = (bf16[128,768]{1,0:T(8,128)(2,1)S(1)}, bf16[128,768]{1,0:T(8,128)(2,1)S(1)}, u32[]{:S(2)}, u32[]{:S(2)}) collective-permute-start(bf16[128,768]{1,0:T(8,128)(2,1)S(1)} %pad_maximum_fusion.2), channel_id=1, source_target_pairs={{0,16},{4,20},{8,24},{12,28},{16,0},{20,4},{24,8},{28,12},{1,17},{... | collective-permute-start | bytes 589832 | tf_op jit(solution)/shard_map/ppermute | solution.py:265
  57.0 11.8 %collective-permute-start.16 = (bf16[128,768]{1,0:T(8,128)(2,1)S(1)}, bf16[128,768]{1,0:T(8,128)(2,1)S(1)}, u32[]{:S(2)}, u32[]{:S(2)}) collective-permute-start(bf16[128,768]{1,0:T(8,128)(2,1)S(1)} %pad_maximum_fusion.2), channel_id=1, source_target_pairs={{0,24},{4,28},{8,16},{12,20},{16,8},{20,12},{24,0},{28,4},{1,25},{... | collective-permute-start | bytes 589832 | tf_op jit(solution)/shard_map/ppermute | solution.py:265
  62.8 1.8 %collective-permute-start.20 = (bf16[256,768]{1,0:T(8,128)(2,1)S(1)}, bf16[256,768]{1,0:T(8,128)(2,1)S(1)}, u32[]{:S(2)}, u32[]{:S(2)}) collective-permute-start(bf16[256,768]{1,0:T(8,128)(2,1)S(1)} %constant_dynamic-update-slice_fusion), channel_id=1, source_target_pairs={{0,4},{4,0},{8,12},{12,8},{16,20},{20,16},{24,28},{28,24},{1,5},{5... | collective-permute-start | bytes 1179656 | tf_op jit(solution)/shard_map/ppermute | solution.py:265
  65.8 1.8 %collective-permute-start.21 = (bf16[256,768]{1,0:T(8,128)(2,1)S(1)}, bf16[256,768]{1,0:T(8,128)(2,1)S(1)}, u32[]{:S(2)}, u32[]{:S(2)}) collective-permute-start(bf16[256,768]{1,0:T(8,128)(2,1)S(1)} %constant_dynamic-update-slice_fusion.2), channel_id=1, source_target_pairs={{0,4},{4,0},{8,12},{12,8},{16,20},{20,16},{24,28},{28,24},{1,5},{5... | collective-permute-start | bytes 1179656 | tf_op jit(solution)/shard_map/ppermute | solution.py:265
  68.8 1.8 %collective-permute-start.22 = (bf16[256,768]{1,0:T(8,128)(2,1)S(1)}, bf16[256,768]{1,0:T(8,128)(2,1)S(1)}, u32[]{:S(2)}, u32[]{:S(2)}) collective-permute-start(bf16[256,768]{1,0:T(8,128)(2,1)S(1)} %constant_dynamic-update-slice_fusion.4), channel_id=1, source_target_pairs={{0,4},{4,0},{8,12},{12,8},{16,20},{20,16},{24,28},{28,24},{1,5},{5... | collective-permute-start | bytes 1179656 | tf_op jit(solution)/shard_map/ppermute | solution.py:265
  72.9 1.8 %collective-permute-start.23 = (bf16[256,768]{1,0:T(8,128)(2,1)S(1)}, bf16[256,768]{1,0:T(8,128)(2,1)S(1)}, u32[]{:S(2)}, u32[]{:S(2)}) collective-permute-start(bf16[256,768]{1,0:T(8,128)(2,1)S(1)} %fusion.75), channel_id=1, source_target_pairs={{0,4},{4,0},{8,12},{12,8},{16,20},{20,16},{24,28},{28,24},{1,5},{5... | collective-permute-start | bytes 1179656 | tf_op jit(solution)/shard_map/ppermute | solution.py:265
  73.7 1.8 %collective-permute-start.24 = (bf16[256,768]{1,0:T(8,128)(2,1)S(1)}, bf16[256,768]{1,0:T(8,128)(2,1)S(1)}, u32[]{:S(2)}, u32[]{:S(2)}) collective-permute-start(bf16[256,768]{1,0:T(8,128)(2,1)S(1)} %fusion.78), channel_id=1, source_target_pairs={{0,4},{4,0},{8,12},{12,8},{16,20},{20,16},{24,28},{28,24},{1,5},{5... | collective-permute-start | bytes 1179656 | tf_op jit(solution)/shard_map/ppermute | solution.py:265
  76.8 5.2 %collective-permute-start.28 = (bf16[256,768]{1,0:T(8,128)(2,1)S(1)}, bf16[256,768]{1,0:T(8,128)(2,1)S(1)}, u32[]{:S(2)}, u32[]{:S(2)}) collective-permute-start(bf16[256,768]{1,0:T(8,128)(2,1)S(1)} %fusion.84), channel_id=1, source_target_pairs={{0,4},{4,0},{8,12},{12,8},{16,20},{20,16},{24,28},{28,24},{1,5},{5... | collective-permute-start | bytes 1179656 | tf_op jit(solution)/shard_map/ppermute | solution.py:265
  77.8 4.9 %collective-permute-start.25 = (bf16[256,768]{1,0:T(8,128)(2,1)S(1)}, bf16[256,768]{1,0:T(8,128)(2,1)S(1)}, u32[]{:S(2)}, u32[]{:S(2)}) collective-permute-start(bf16[256,768]{1,0:T(8,128)(2,1)S(1)} %fusion.81), channel_id=1, source_target_pairs={{0,4},{4,0},{8,12},{12,8},{16,20},{20,16},{24,28},{28,24},{1,5},{5... | collective-permute-start | bytes 1179656 | tf_op jit(solution)/shard_map/ppermute | solution.py:265
  78.0 16.3 %collective-permute-start.27 = (bf16[192,768]{1,0:T(8,128)(2,1)S(1)}, bf16[192,768]{1,0:T(8,128)(2,1)S(1)}, u32[]{:S(2)}, u32[]{:S(2)}) collective-permute-start(bf16[192,768]{1,0:T(8,128)(2,1)S(1)} %slice.172), channel_id=1, source_target_pairs={{0,16},{4,20},{8,24},{12,28},{16,0},{20,4},{24,8},{28,12},{1,17},{... | collective-permute-start | bytes 884744 | tf_op jit(solution)/shard_map/ppermute | solution.py:265
  80.4 13.9 %collective-permute-start.26 = (bf16[192,768]{1,0:T(8,128)(2,1)S(1)}, bf16[192,768]{1,0:T(8,128)(2,1)S(1)}, u32[]{:S(2)}, u32[]{:S(2)}) collective-permute-start(bf16[192,768]{1,0:T(8,128)(2,1)S(1)} %slice.170), channel_id=1, source_target_pairs={{0,24},{4,28},{8,16},{12,20},{16,8},{20,12},{24,0},{28,4},{1,25},{... | collective-permute-start | bytes 884744 | tf_op jit(solution)/shard_map/ppermute | solution.py:265
  82.6 21.3 %copy-start.1 = (f32[96,2]{0,1:T(2,128)S(1)}, f32[96,2]{0,1:T(2,128)}, u32[]{:S(2)}) copy-start(f32[96,2]{0,1:T(2,128)} %param.22) | copy-start | bytes 2308
  82.6 12.9 %collective-permute-start.29 = (bf16[192,768]{1,0:T(8,128)(2,1)S(1)}, bf16[192,768]{1,0:T(8,128)(2,1)S(1)}, u32[]{:S(2)}, u32[]{:S(2)}) collective-permute-start(bf16[192,768]{1,0:T(8,128)(2,1)S(1)} %slice.175), channel_id=1, source_target_pairs={{0,8},{4,12},{8,0},{12,4},{16,24},{20,28},{24,16},{28,20},{1,9},{5... | collective-permute-start | bytes 884744 | tf_op jit(solution)/shard_map/ppermute | solution.py:265
  95.7 7.7 %collective-permute-start.30 = (bf16[64,768]{1,0:T(8,128)(2,1)S(1)}, bf16[64,768]{1,0:T(8,128)(2,1)S(1)}, u32[]{:S(2)}, u32[]{:S(2)}) collective-permute-start(bf16[64,768]{1,0:T(8,128)(2,1)S(1)} %get-tuple-element.169), channel_id=1, source_target_pairs={{0,1},{1,0},{2,3},{3,2},{4,5},{5,4},{6,7},{7,6},{8,9},{9,8},{10,11... | collective-permute-start | bytes 294920 | tf_op jit(solution)/shard_map/ppermute | solution.py:265
  97.8 10.1 %collective-permute-start.31 = (bf16[64,768]{1,0:T(8,128)(2,1)S(1)}, bf16[64,768]{1,0:T(8,128)(2,1)S(1)}, u32[]{:S(2)}, u32[]{:S(2)}) collective-permute-start(bf16[64,768]{1,0:T(8,128)(2,1)S(1)} %get-tuple-element.168), channel_id=1, source_target_pairs={{0,2},{1,3},{2,0},{3,1},{4,6},{5,7},{6,4},{7,5},{8,10},{9,11},{10,... | collective-permute-start | bytes 294920 | tf_op jit(solution)/shard_map/ppermute | solution.py:265
  99.0 8.9 %collective-permute-start.32 = (bf16[64,768]{1,0:T(8,128)(2,1)S(1)}, bf16[64,768]{1,0:T(8,128)(2,1)S(1)}, u32[]{:S(2)}, u32[]{:S(2)}) collective-permute-start(bf16[64,768]{1,0:T(8,128)(2,1)S(1)} %get-tuple-element.167), channel_id=1, source_target_pairs={{0,3},{1,2},{2,1},{3,0},{4,7},{5,6},{6,5},{7,4},{8,11},{9,10},{10,... | collective-permute-start | bytes 294920 | tf_op jit(solution)/shard_map/ppermute | solution.py:265
  100.4 7.6 %collective-permute-start.33 = (bf16[64,768]{1,0:T(8,128)(2,1)S(1)}, bf16[64,768]{1,0:T(8,128)(2,1)S(1)}, u32[]{:S(2)}, u32[]{:S(2)}) collective-permute-start(bf16[64,768]{1,0:T(8,128)(2,1)S(1)} %slice.169), channel_id=1, source_target_pairs={{0,24},{4,28},{8,16},{12,20},{16,8},{20,12},{24,0},{28,4},{1,25},{... | collective-permute-start | bytes 294920 | tf_op jit(solution)/shard_map/ppermute | solution.py:265
  102.7 5.2 %collective-permute-start.34 = (bf16[64,768]{1,0:T(8,128)(2,1)S(1)}, bf16[64,768]{1,0:T(8,128)(2,1)S(1)}, u32[]{:S(2)}, u32[]{:S(2)}) collective-permute-start(bf16[64,768]{1,0:T(8,128)(2,1)S(1)} %slice.171), channel_id=1, source_target_pairs={{0,16},{4,20},{8,24},{12,28},{16,0},{20,4},{24,8},{28,12},{1,17},{... | collective-permute-start | bytes 294920 | tf_op jit(solution)/shard_map/ppermute | solution.py:265
  103.4 4.6 %collective-permute-start.35 = (bf16[64,768]{1,0:T(8,128)(2,1)S(1)}, bf16[64,768]{1,0:T(8,128)(2,1)S(1)}, u32[]{:S(2)}, u32[]{:S(2)}) collective-permute-start(bf16[64,768]{1,0:T(8,128)(2,1)S(1)} %slice.176), channel_id=1, source_target_pairs={{0,8},{4,12},{8,0},{12,4},{16,24},{20,28},{24,16},{28,20},{1,9},{5... | collective-permute-start | bytes 294920 | tf_op jit(solution)/shard_map/ppermute | solution.py:265
